TPU v7x, 32 devices: a whole 2x2x4 slice. The times are simulated.
32 devices in a mesh: ctx: 16 (over z, x, core), tp: 2 (over y).
Axes of the slice: x: 2, y: 2, z: 4, core: 2. Of those that a mesh axis runs over, the one named last changes fastest.
Arguments:
- projected: bfloat16 [3, 4096, 8192], P(None, 'ctx', 'tp'), may hold values from -6 to 6
- short_weight: float32 [3, 3, 8192], P(None, None, 'tp'), may hold values from -4 to 4
- rate: float32 [8192, 16], P('tp'), may hold values from 0.00012207031 to 0.05
- residue: float32 [8192, 16], P('tp'), may hold values from -5 to 5
- skip: float32 [8192], P('tp'), may hold values from -4 to 4
- w_out: bfloat16 [8192, 4096], P('tp'), may hold values from -0.09375 to 0.09375
Outputs:
- layer_out: bfloat16 [4096, 4096], P('ctx', 'tp')
All inputs are finite; a program needn't handle non-finite values.
Results may differ from a plain program's by a relative error of at most 0.011.
Values may be sent and summed in bfloat16 or wider, within the bound.
A program may use at most 256 MiB of HBM per device.

v0:
```python
import math

import jax
import jax.numpy as jnp
from jax import lax
from jax.sharding import PartitionSpec as P

two_pi = 2.0 * math.pi


def passed_along(value, axis, steps):
    count = lax.axis_size(axis)
    initial, last = (max(0, -steps), min(count, count - steps))
    return lax.ppermute(value, axis, [(source, source + steps) for source in range(initial, last)])


def dft_tables(count_a, count_b):
    span_a = 2 * count_a
    freq_a = jnp.arange(span_a, dtype=jnp.int32)
    pos_a = jnp.arange(count_a, dtype=jnp.int32)
    pos_b = jnp.arange(count_b, dtype=jnp.int32)
    angle_a = two_pi / span_a * (freq_a[:, None] * pos_a[None, :] % span_a).astype(jnp.float32)
    angle_b = two_pi / count_b * (pos_b[:, None] * pos_b[None, :] % count_b).astype(jnp.float32)
    return (
        jnp.cos(angle_a).astype(jnp.bfloat16),
        jnp.sin(angle_a).astype(jnp.bfloat16),
        jnp.cos(angle_b).astype(jnp.bfloat16),
        jnp.sin(angle_b).astype(jnp.bfloat16),
    )


def twist_tables(rows_k, cols_b, full_len):
    angle = two_pi / full_len * (rows_k[:, None] * cols_b[None, :] % full_len).astype(jnp.float32)
    return (jnp.cos(angle), jnp.sin(angle))


def filter_spectrum(frequency, rate, residue, length):
    full_len = 2 * length
    mode_count = rate.shape[1]
    steps_f = (frequency % full_len).astype(jnp.float32)
    half_sin = jnp.sin(math.pi / full_len * steps_f)[:, None]
    full_sin = jnp.sin(two_pi / full_len * steps_f)[:, None]
    parity = (1 - 2 * (frequency % 2)).astype(jnp.float32)[:, None]

    def add_mode(mode_index, partial_value):
        rates_now = lax.dynamic_index_in_dim(rate, mode_index, 1, keepdims=False)[None, :]
        mode_weight = lax.dynamic_index_in_dim(residue, mode_index, 1, keepdims=False)[None, :]
        damping = jnp.exp(-rates_now)
        denom_re = -jnp.expm1(-rates_now) + 2.0 * damping * half_sin * half_sin
        denom_im = damping * full_sin
        numerator = (
            mode_weight
            * jnp.sqrt(2.0 * rates_now / mode_count)
            * (1.0 - jnp.exp(-rates_now * length) * parity)
        )
        factor = numerator / (denom_re * denom_re + denom_im * denom_im)
        return (partial_value[0] + factor * denom_re, partial_value[1] - factor * denom_im)

    grid_shape = (frequency.shape[0], rate.shape[0])
    initial = (jnp.zeros(grid_shape, jnp.float32), jnp.zeros(grid_shape, jnp.float32))
    return lax.fori_loop(0, mode_count, add_mode, initial)


def sequence_conv(product, rate, residue):
    count_a = lax.axis_size("ctx")
    device_rank = lax.axis_index("ctx")
    count_b = product.shape[0]
    channels = product.shape[1]
    span_a = 2 * count_a
    full_len = span_a * count_b
    length = count_a * count_b
    slab_len = count_b // count_a
    cos_a, sin_a, cos_b, sin_b = dft_tables(count_a, count_b)
    own_pos = device_rank * slab_len + jnp.arange(slab_len, dtype=jnp.int32)
    fwd_cos, fwd_sin = twist_tables(jnp.arange(span_a, dtype=jnp.int32), own_pos, full_len)
    fwd_cos = fwd_cos[:, :, None]
    fwd_sin = fwd_sin[:, :, None]
    inputs = lax.all_to_all(product[None], "ctx", split_axis=1, concat_axis=0, tiled=True)
    real_part = jnp.einsum("ka,abc->kbc", cos_a, inputs, preferred_element_type=jnp.float32)
    imag_part = -jnp.einsum("ka,abc->kbc", sin_a, inputs, preferred_element_type=jnp.float32)
    section_re = (real_part * fwd_cos + imag_part * fwd_sin).astype(jnp.bfloat16)
    section_im = (imag_part * fwd_cos - real_part * fwd_sin).astype(jnp.bfloat16)
    section_re, section_im = (section_re, section_im)
    part_re = lax.all_to_all(section_re, "ctx", split_axis=0, concat_axis=1, tiled=True)
    part_im = lax.all_to_all(section_im, "ctx", split_axis=0, concat_axis=1, tiled=True)
    spec_re = jnp.einsum(
        "kbc,bm->kmc", part_re, cos_b, preferred_element_type=jnp.float32
    ) + jnp.einsum("kbc,bm->kmc", part_im, sin_b, preferred_element_type=jnp.float32)
    spec_im = jnp.einsum(
        "kbc,bm->kmc", part_im, cos_b, preferred_element_type=jnp.float32
    ) - jnp.einsum("kbc,bm->kmc", part_re, sin_b, preferred_element_type=jnp.float32)
    spec_re, spec_im = (spec_re, spec_im)
    own_freq = device_rank * 2 + jnp.arange(2, dtype=jnp.int32)
    frequency = (
        own_freq[:, None] + span_a * jnp.arange(count_b, dtype=jnp.int32)[None, :]
    ).reshape(-1)
    resp_re, resp_im = filter_spectrum(frequency, rate, residue, length)
    resp_re = resp_re.reshape(2, count_b, channels)
    resp_im = resp_im.reshape(2, count_b, channels)
    filt_re = (spec_re * resp_re - spec_im * resp_im).astype(jnp.bfloat16)
    filt_im = (spec_re * resp_im + spec_im * resp_re).astype(jnp.bfloat16)
    back_re = jnp.einsum(
        "kmc,mb->kbc", filt_re, cos_b, preferred_element_type=jnp.float32
    ) - jnp.einsum("kmc,mb->kbc", filt_im, sin_b, preferred_element_type=jnp.float32)
    back_im = jnp.einsum(
        "kmc,mb->kbc", filt_re, sin_b, preferred_element_type=jnp.float32
    ) + jnp.einsum("kmc,mb->kbc", filt_im, cos_b, preferred_element_type=jnp.float32)
    inv_cos, inv_sin = twist_tables(own_freq, jnp.arange(count_b, dtype=jnp.int32), full_len)
    inv_cos = inv_cos[:, :, None]
    inv_sin = inv_sin[:, :, None]
    twist_re = (back_re * inv_cos - back_im * inv_sin).astype(jnp.bfloat16)
    twist_im = (back_im * inv_cos + back_re * inv_sin).astype(jnp.bfloat16)
    part_re = lax.all_to_all(twist_re, "ctx", split_axis=1, concat_axis=0, tiled=True)
    part_im = lax.all_to_all(twist_im, "ctx", split_axis=1, concat_axis=0, tiled=True)
    summed = jnp.einsum(
        "ka,kbc->abc", cos_a, part_re, preferred_element_type=jnp.float32
    ) - jnp.einsum("ka,kbc->abc", sin_a, part_im, preferred_element_type=jnp.float32)
    convolved = (summed * (1.0 / full_len)).astype(jnp.bfloat16)
    restored = lax.all_to_all(convolved, "ctx", split_axis=0, concat_axis=1, tiled=True)
    return restored[0]


def on_device(projected, short_weight, rate, residue, skip, w_out):
    rim_rows = passed_along(projected[:, -2:, :], "ctx", 1)
    padded = jnp.concatenate([rim_rows, projected], axis=1).astype(jnp.float32)
    mixed = (
        short_weight[:, 0][:, None, :] * padded[:, 2:]
        + short_weight[:, 1][:, None, :] * padded[:, 1:-1]
        + short_weight[:, 2][:, None, :] * padded[:, :-2]
    )
    features = mixed.astype(jnp.bfloat16)
    product = (features[1].astype(jnp.float32) * features[2].astype(jnp.float32)).astype(
        jnp.bfloat16
    )
    convolved = sequence_conv(product, rate, residue)
    gated = (
        features[0].astype(jnp.float32)
        * (convolved.astype(jnp.float32) + skip[None, :] * product.astype(jnp.float32))
    ).astype(jnp.bfloat16)
    summed = lax.psum_scatter(
        lax.dot_general(
            w_out, gated, (((0,), (1,)), ((), ())), preferred_element_type=jnp.float32
        ).astype(jnp.bfloat16),
        "tp",
        scatter_dimension=0,
        tiled=True,
    ).astype(jnp.float32)
    return summed.T.astype(jnp.bfloat16)


def solution(mesh):
    return jax.shard_map(
        on_device,
        mesh=mesh,
        in_specs=(
            P(None, "ctx", "tp"),
            P(None, None, "tp"),
            P("tp", None),
            P("tp", None),
            P("tp"),
            P("tp", None),
        ),
        out_specs=P("ctx", "tp"),
        check_vma=False,
    )
```

profile of v0, /device:TPU:0, one launch (start us, length us, event | category | flops | bytes accessed | tf_op | source)
XLA Modules:
  0.0 840.1 jit_solution(2754695889861566477)
XLA Ops:
  32.9 13.5 %reduce = bf16[256,4096]{1,0:T(8,128)(2,1)S(1)} reduce(bf16[256,1,4096]{2,1,0:T(2,128)(2,1)} %bitcast.164, bf16[]{:T(256)} %broadcast.452), dimensions={1}, to_apply=%bitcast.135.reduce_sub_computation | reduce | bytes 4194306
  49.3 9.1 %all-to-all-start = ((bf16[16,2,32768]{2,1,0:T(2,128)(2,1)}), bf16[16,2,32768]{2,1,0:T(2,128)(2,1)S(1)}, u32[]{:S(2)}, u32[]{:S(2)}) async-start(bf16[16,2,32768]{2,1,0:T(2,128)(2,1)} %reshape.359), calls=%async_computation | async-start | bytes 4194304 | tf_op jit(solution)/shard_map/all_to_all | solution.py:78
  58.5 40.9 %all-to-all-done = bf16[16,2,32768]{2,1,0:T(2,128)(2,1)S(1)} async-done(((bf16[16,2,32768]{2,1,0:T(2,128)(2,1)}), bf16[16,2,32768]{2,1,0:T(2,128)(2,1)S(1)}, u32[]{:S(2)}, u32[]{:S(2)}) %all-to-all-start) | async-done | bytes 2097184 | tf_op jit(solution)/shard_map/all_to_all | solution.py:78
  124.0 11.3 %all-to-all-start.1 = ((bf16[32,16,4096]{2,1,0:T(8,128)(2,1)}), bf16[32,16,4096]{2,1,0:T(8,128)(2,1)}, u32[]{:S(2)}, u32[]{:S(2)}) async-start(bf16[32,16,4096]{2,1,0:T(8,128)(2,1)} %copy.21), calls=%async_computation.1 | async-start | bytes 8388608 | tf_op jit(solution)/shard_map/all_to_all | solution.py:84
  141.8 71.1 %all-to-all-done.1 = bf16[32,16,4096]{2,1,0:T(8,128)(2,1)} async-done(((bf16[32,16,4096]{2,1,0:T(8,128)(2,1)}), bf16[32,16,4096]{2,1,0:T(8,128)(2,1)}, u32[]{:S(2)}, u32[]{:S(2)}) %all-to-all-start.1) | async-done | bytes 4194336 | tf_op jit(solution)/shard_map/all_to_all | solution.py:84
  212.9 19.9 %all-to-all-start.2 = ((bf16[32,16,4096]{2,1,0:T(8,128)(2,1)}), bf16[32,16,4096]{2,1,0:T(8,128)(2,1)}, u32[]{:S(2)}, u32[]{:S(2)}) async-start(bf16[32,16,4096]{2,1,0:T(8,128)(2,1)} %copy.23), calls=%async_computation.2 | async-start | bytes 8388608 | tf_op jit(solution)/shard_map/all_to_all | solution.py:85
  232.9 212.8 %while.20 = (s32[]{:T(128)}, f32[512,4096]{1,0:T(8,128)}, f32[512,4096]{1,0:T(8,128)}, f32[4096,16]{0,1:T(8,128)}, f32[4096,16]{0,1:T(8,128)}, /*index=5*/s32[256]{0:T(256)S(1)}, s32[2]{0:T(128)S(1)}, s32[]{:T(128)}, s32[]{:T(128)}) while((s32[]{:T(128)}, f32[512,4096]{1,0:T(8,128)}, f32[512,4096]{1,0:T(8,128)}, ...), condition=%wide.region_1.2_spmd.clone.clone.clone, body=%wide.region_0.1_spmd.clone.clone.clone.sunk | while | flops 35691008 | bytes 33795192 | solution.py:61
  234.3 8.7 %fusion.148 = (f32[512,4096]{1,0:T(8,128)}, f32[512,4096]{1,0:T(8,128)}) fusion(f32[512,4096]{1,0:T(8,128)} %get-tuple-element.402, f32[512]{0:T(512)S(1)} %bitcast.177, f32[4096]{0:T(1024)S(1)} %bitcast.169, f32[512]{0:T(512)S(1)} %bitcast.178, f32[4096]{0:T(1024)S(1)} %broadcast_multiply_fusion.2, f32[4096]{0:T(1024)S(1)} %bitcast.172, ...), kind=kLoop, calls=%fused_computation.7.clone.1 | loop fusion | flops 35651584 | bytes 33642496 | tf_op jit(solution)/shard_map/while/body/eval_jaxpr/sub | solution.py:57
  244.4 12.1 %fusion.148 = (f32[512,4096]{1,0:T(8,128)}, f32[512,4096]{1,0:T(8,128)}) fusion(f32[512,4096]{1,0:T(8,128)} %get-tuple-element.402, f32[512]{0:T(512)S(1)} %bitcast.177, f32[4096]{0:T(1024)S(1)} %bitcast.169, f32[512]{0:T(512)S(1)} %bitcast.178, f32[4096]{0:T(1024)S(1)} %broadcast_multiply_fusion.2, f32[4096]{0:T(1024)S(1)} %bitcast.172, ...), kind=kLoop, calls=%fused_computation.7.clone.1 | loop fusion | flops 35651584 | bytes 33642496 | tf_op jit(solution)/shard_map/while/body/eval_jaxpr/sub | solution.py:57
  257.9 12.1 %fusion.148 = (f32[512,4096]{1,0:T(8,128)}, f32[512,4096]{1,0:T(8,128)}) fusion(f32[512,4096]{1,0:T(8,128)} %get-tuple-element.402, f32[512]{0:T(512)S(1)} %bitcast.177, f32[4096]{0:T(1024)S(1)} %bitcast.169, f32[512]{0:T(512)S(1)} %bitcast.178, f32[4096]{0:T(1024)S(1)} %broadcast_multiply_fusion.2, f32[4096]{0:T(1024)S(1)} %bitcast.172, ...), kind=kLoop, calls=%fused_computation.7.clone.1 | loop fusion | flops 35651584 | bytes 33642496 | tf_op jit(solution)/shard_map/while/body/eval_jaxpr/sub | solution.py:57
  271.4 12.1 %fusion.148 = (f32[512,4096]{1,0:T(8,128)}, f32[512,4096]{1,0:T(8,128)}) fusion(f32[512,4096]{1,0:T(8,128)} %get-tuple-element.402, f32[512]{0:T(512)S(1)} %bitcast.177, f32[4096]{0:T(1024)S(1)} %bitcast.169, f32[512]{0:T(512)S(1)} %bitcast.178, f32[4096]{0:T(1024)S(1)} %broadcast_multiply_fusion.2, f32[4096]{0:T(1024)S(1)} %bitcast.172, ...), kind=kLoop, calls=%fused_computation.7.clone.1 | loop fusion | flops 35651584 | bytes 33642496 | tf_op jit(solution)/shard_map/while/body/eval_jaxpr/sub | solution.py:57
  284.9 12.1 %fusion.148 = (f32[512,4096]{1,0:T(8,128)}, f32[512,4096]{1,0:T(8,128)}) fusion(f32[512,4096]{1,0:T(8,128)} %get-tuple-element.402, f32[512]{0:T(512)S(1)} %bitcast.177, f32[4096]{0:T(1024)S(1)} %bitcast.169, f32[512]{0:T(512)S(1)} %bitcast.178, f32[4096]{0:T(1024)S(1)} %broadcast_multiply_fusion.2, f32[4096]{0:T(1024)S(1)} %bitcast.172, ...), kind=kLoop, calls=%fused_computation.7.clone.1 | loop fusion | flops 35651584 | bytes 33642496 | tf_op jit(solution)/shard_map/while/body/eval_jaxpr/sub | solution.py:57
  298.4 12.1 %fusion.148 = (f32[512,4096]{1,0:T(8,128)}, f32[512,4096]{1,0:T(8,128)}) fusion(f32[512,4096]{1,0:T(8,128)} %get-tuple-element.402, f32[512]{0:T(512)S(1)} %bitcast.177, f32[4096]{0:T(1024)S(1)} %bitcast.169, f32[512]{0:T(512)S(1)} %bitcast.178, f32[4096]{0:T(1024)S(1)} %broadcast_multiply_fusion.2, f32[4096]{0:T(1024)S(1)} %bitcast.172, ...), kind=kLoop, calls=%fused_computation.7.clone.1 | loop fusion | flops 35651584 | bytes 33642496 | tf_op jit(solution)/shard_map/while/body/eval_jaxpr/sub | solution.py:57
  311.9 12.1 %fusion.148 = (f32[512,4096]{1,0:T(8,128)}, f32[512,4096]{1,0:T(8,128)}) fusion(f32[512,4096]{1,0:T(8,128)} %get-tuple-element.402, f32[512]{0:T(512)S(1)} %bitcast.177, f32[4096]{0:T(1024)S(1)} %bitcast.169, f32[512]{0:T(512)S(1)} %bitcast.178, f32[4096]{0:T(1024)S(1)} %broadcast_multiply_fusion.2, f32[4096]{0:T(1024)S(1)} %bitcast.172, ...), kind=kLoop, calls=%fused_computation.7.clone.1 | loop fusion | flops 35651584 | bytes 33642496 | tf_op jit(solution)/shard_map/while/body/eval_jaxpr/sub | solution.py:57
  325.5 12.1 %fusion.148 = (f32[512,4096]{1,0:T(8,128)}, f32[512,4096]{1,0:T(8,128)}) fusion(f32[512,4096]{1,0:T(8,128)} %get-tuple-element.402, f32[512]{0:T(512)S(1)} %bitcast.177, f32[4096]{0:T(1024)S(1)} %bitcast.169, f32[512]{0:T(512)S(1)} %bitcast.178, f32[4096]{0:T(1024)S(1)} %broadcast_multiply_fusion.2, f32[4096]{0:T(1024)S(1)} %bitcast.172, ...), kind=kLoop, calls=%fused_computation.7.clone.1 | loop fusion | flops 35651584 | bytes 33642496 | tf_op jit(solution)/shard_map/while/body/eval_jaxpr/sub | solution.py:57
  339.0 12.1 %fusion.148 = (f32[512,4096]{1,0:T(8,128)}, f32[512,4096]{1,0:T(8,128)}) fusion(f32[512,4096]{1,0:T(8,128)} %get-tuple-element.402, f32[512]{0:T(512)S(1)} %bitcast.177, f32[4096]{0:T(1024)S(1)} %bitcast.169, f32[512]{0:T(512)S(1)} %bitcast.178, f32[4096]{0:T(1024)S(1)} %broadcast_multiply_fusion.2, f32[4096]{0:T(1024)S(1)} %bitcast.172, ...), kind=kLoop, calls=%fused_computation.7.clone.1 | loop fusion | flops 35651584 | bytes 33642496 | tf_op jit(solution)/shard_map/while/body/eval_jaxpr/sub | solution.py:57
  352.5 12.1 %fusion.148 = (f32[512,4096]{1,0:T(8,128)}, f32[512,4096]{1,0:T(8,128)}) fusion(f32[512,4096]{1,0:T(8,128)} %get-tuple-element.402, f32[512]{0:T(512)S(1)} %bitcast.177, f32[4096]{0:T(1024)S(1)} %bitcast.169, f32[512]{0:T(512)S(1)} %bitcast.178, f32[4096]{0:T(1024)S(1)} %broadcast_multiply_fusion.2, f32[4096]{0:T(1024)S(1)} %bitcast.172, ...), kind=kLoop, calls=%fused_computation.7.clone.1 | loop fusion | flops 35651584 | bytes 33642496 | tf_op jit(solution)/shard_map/while/body/eval_jaxpr/sub | solution.py:57
  366.0 12.1 %fusion.148 = (f32[512,4096]{1,0:T(8,128)}, f32[512,4096]{1,0:T(8,128)}) fusion(f32[512,4096]{1,0:T(8,128)} %get-tuple-element.402, f32[512]{0:T(512)S(1)} %bitcast.177, f32[4096]{0:T(1024)S(1)} %bitcast.169, f32[512]{0:T(512)S(1)} %bitcast.178, f32[4096]{0:T(1024)S(1)} %broadcast_multiply_fusion.2, f32[4096]{0:T(1024)S(1)} %bitcast.172, ...), kind=kLoop, calls=%fused_computation.7.clone.1 | loop fusion | flops 35651584 | bytes 33642496 | tf_op jit(solution)/shard_map/while/body/eval_jaxpr/sub | solution.py:57
  379.5 12.1 %fusion.148 = (f32[512,4096]{1,0:T(8,128)}, f32[512,4096]{1,0:T(8,128)}) fusion(f32[512,4096]{1,0:T(8,128)} %get-tuple-element.402, f32[512]{0:T(512)S(1)} %bitcast.177, f32[4096]{0:T(1024)S(1)} %bitcast.169, f32[512]{0:T(512)S(1)} %bitcast.178, f32[4096]{0:T(1024)S(1)} %broadcast_multiply_fusion.2, f32[4096]{0:T(1024)S(1)} %bitcast.172, ...), kind=kLoop, calls=%fused_computation.7.clone.1 | loop fusion | flops 35651584 | bytes 33642496 | tf_op jit(solution)/shard_map/while/body/eval_jaxpr/sub | solution.py:57
  393.0 12.1 %fusion.148 = (f32[512,4096]{1,0:T(8,128)}, f32[512,4096]{1,0:T(8,128)}) fusion(f32[512,4096]{1,0:T(8,128)} %get-tuple-element.402, f32[512]{0:T(512)S(1)} %bitcast.177, f32[4096]{0:T(1024)S(1)} %bitcast.169, f32[512]{0:T(512)S(1)} %bitcast.178, f32[4096]{0:T(1024)S(1)} %broadcast_multiply_fusion.2, f32[4096]{0:T(1024)S(1)} %bitcast.172, ...), kind=kLoop, calls=%fused_computation.7.clone.1 | loop fusion | flops 35651584 | bytes 33642496 | tf_op jit(solution)/shard_map/while/body/eval_jaxpr/sub | solution.py:57
  406.5 12.1 %fusion.148 = (f32[512,4096]{1,0:T(8,128)}, f32[512,4096]{1,0:T(8,128)}) fusion(f32[512,4096]{1,0:T(8,128)} %get-tuple-element.402, f32[512]{0:T(512)S(1)} %bitcast.177, f32[4096]{0:T(1024)S(1)} %bitcast.169, f32[512]{0:T(512)S(1)} %bitcast.178, f32[4096]{0:T(1024)S(1)} %broadcast_multiply_fusion.2, f32[4096]{0:T(1024)S(1)} %bitcast.172, ...), kind=kLoop, calls=%fused_computation.7.clone.1 | loop fusion | flops 35651584 | bytes 33642496 | tf_op jit(solution)/shard_map/while/body/eval_jaxpr/sub | solution.py:57
  420.1 12.1 %fusion.148 = (f32[512,4096]{1,0:T(8,128)}, f32[512,4096]{1,0:T(8,128)}) fusion(f32[512,4096]{1,0:T(8,128)} %get-tuple-element.402, f32[512]{0:T(512)S(1)} %bitcast.177, f32[4096]{0:T(1024)S(1)} %bitcast.169, f32[512]{0:T(512)S(1)} %bitcast.178, f32[4096]{0:T(1024)S(1)} %broadcast_multiply_fusion.2, f32[4096]{0:T(1024)S(1)} %bitcast.172, ...), kind=kLoop, calls=%fused_computation.7.clone.1 | loop fusion | flops 35651584 | bytes 33642496 | tf_op jit(solution)/shard_map/while/body/eval_jaxpr/sub | solution.py:57
  433.6 12.1 %fusion.148 = (f32[512,4096]{1,0:T(8,128)}, f32[512,4096]{1,0:T(8,128)}) fusion(f32[512,4096]{1,0:T(8,128)} %get-tuple-element.402, f32[512]{0:T(512)S(1)} %bitcast.177, f32[4096]{0:T(1024)S(1)} %bitcast.169, f32[512]{0:T(512)S(1)} %bitcast.178, f32[4096]{0:T(1024)S(1)} %broadcast_multiply_fusion.2, f32[4096]{0:T(1024)S(1)} %bitcast.172, ...), kind=kLoop, calls=%fused_computation.7.clone.1 | loop fusion | flops 35651584 | bytes 33642496 | tf_op jit(solution)/shard_map/while/body/eval_jaxpr/sub | solution.py:57
  469.5 16.6 %fusion.24 = (bf16[2,256,4096]{2,1,0:T(8,128)(2,1)}, bf16[2,256,4096]{2,1,0:T(8,128)(2,1)S(1)}) fusion(f32[2,256,4096]{2,1,0:T(8,128)} %bitcast.154, f32[2,256,4096]{2,1,0:T(8,128)} %bitcast.155, f32[256,2,4096]{2,0,1:T(8,128)} %convolution_add_fusion.1, f32[256,2,4096]{2,0,1:T(8,128)} %fusion.54, bf16[2,256,4096]{2,1,0:T(8,128)(2,1)} %bitcast.159), kind=kOutput, calls=%fused_computation.47 | convolution fusion | flops 1093599232 | bytes 46137344 | tf_op jit(solution)/shard_map/kbc,bm->kmc/dot_general | solution.py:91
  527.3 69.1 %all-to-all-done.3 = bf16[2,256,4096]{2,0,1:T(2,128)(2,1)} async-done(((bf16[2,256,4096]{2,0,1:T(2,128)(2,1)}), bf16[2,256,4096]{2,0,1:T(2,128)(2,1)}, u32[]{:S(2)}, u32[]{:S(2)}) %all-to-all-start.3) | async-done | bytes 4194336 | tf_op jit(solution)/shard_map/all_to_all | solution.py:113
  596.5 19.7 %all-to-all-start.4 = ((bf16[2,256,4096]{2,0,1:T(2,128)(2,1)}), bf16[2,256,4096]{2,0,1:T(2,128)(2,1)}, u32[]{:S(2)}, u32[]{:S(2)}) async-start(bf16[2,256,4096]{2,0,1:T(2,128)(2,1)} %copy.27), calls=%async_computation.4 | async-start | bytes 8388608 | tf_op jit(solution)/shard_map/all_to_all | solution.py:114
  616.4 10.1 %copy.48 = bf16[2,16,16,4096]{3,0,1,2:T(2,128)(2,1)} copy(bf16[2,16,16,4096]{3,0,2,1:T(2,128)(2,1)} %bitcast.19) | data formatting | bytes 8388608 | tf_op jit(solution)/shard_map/all_to_all | solution.py:113
  638.6 55.3 %all-to-all-done.4 = bf16[2,256,4096]{2,0,1:T(2,128)(2,1)} async-done(((bf16[2,256,4096]{2,0,1:T(2,128)(2,1)}), bf16[2,256,4096]{2,0,1:T(2,128)(2,1)}, u32[]{:S(2)}, u32[]{:S(2)}) %all-to-all-start.4) | async-done | bytes 4194336 | tf_op jit(solution)/shard_map/all_to_all | solution.py:114
  693.8 10.1 %copy.47 = bf16[2,16,16,4096]{3,0,1,2:T(2,128)(2,1)} copy(bf16[2,16,16,4096]{3,0,2,1:T(2,128)(2,1)} %bitcast.21) | data formatting | bytes 8388608 | tf_op jit(solution)/shard_map/all_to_all | solution.py:114
  716.6 67.0 %all_to_all.93 = bf16[16,16,4096]{2,1,0:T(8,128)(2,1)S(1)} all-to-all(bf16[16,16,4096]{2,1,0:T(8,128)(2,1)S(1)} %copy.29), channel_id=1, replica_groups=mesh['ctx'=16,'tp'=2] {'ctx'}, dimensions={0} | all-to-all | bytes 4194304 | tf_op jit(solution)/shard_map/all_to_all | solution.py:119
  783.6 16.7 %fusion.27 = bf16[4096,256]{0,1:T(8,128)(2,1)} fusion(bf16[4096,4096]{1,0:T(8,128)(2,1)} %param.13, bf16[256,4096]{1,0:T(8,128)(2,1)S(1)} %bitcast.170, bf16[3,256,4096]{2,1,0:T(8,128)(2,1)} %fusion.15, bf16[1,256,4096]{2,1,0:T(8,128)(2,1)S(1)} %copy-done.4, f32[4096]{0:T(1024)S(1)} %copy-done.5), kind=kOutput, calls=%fused_computation.61 | convolution fusion | flops 8598323200 | bytes 41959424 | tf_op jit(solution)/shard_map/dot_general | solution.py:141
  800.4 32.4 %reduce-scatter.2.cloned.1.call-done = bf16[2048,256]{0,1:T(8,128)(2,1)} async-done(((bf16[4096,256]{0,1:T(8,128)(2,1)}), bf16[2048,256]{0,1:T(8,128)(2,1)}) %reduce-scatter.2.cloned.1.call-update) | async-done | bytes 1048592 | tf_op jit(solution)/shard_map/reduce_scatter | solution.py:140
  (174 shorter events, 171.9 us)
Async XLA Ops:
  7.5 3.8 collective-permute-start
  24.3 1.3 copy-start.3
  49.3 50.2 %all-to-all-start = ((bf16[16,2,32768]{2,1,0:T(2,128)(2,1)}), bf16[16,2,32768]{2,1,0:T(2,128)(2,1)S(1)}, u32[]{:S(2)}, u32[]{:S(2)}) async-start(bf16[16,2,32768]{2,1,0:T(2,128)(2,1)} %reshape.359), calls=%async_computation | async-start | bytes 4194304 | tf_op jit(solution)/shard_map/all_to_all | solution.py:78
  124.0 88.9 %all-to-all-start.1 = ((bf16[32,16,4096]{2,1,0:T(8,128)(2,1)}), bf16[32,16,4096]{2,1,0:T(8,128)(2,1)}, u32[]{:S(2)}, u32[]{:S(2)}) async-start(bf16[32,16,4096]{2,1,0:T(8,128)(2,1)} %copy.21), calls=%async_computation.1 | async-start | bytes 8388608 | tf_op jit(solution)/shard_map/all_to_all | solution.py:84
  212.9 242.8 %all-to-all-start.2 = ((bf16[32,16,4096]{2,1,0:T(8,128)(2,1)}), bf16[32,16,4096]{2,1,0:T(8,128)(2,1)}, u32[]{:S(2)}, u32[]{:S(2)}) async-start(bf16[32,16,4096]{2,1,0:T(8,128)(2,1)} %copy.23), calls=%async_computation.2 | async-start | bytes 8388608 | tf_op jit(solution)/shard_map/all_to_all | solution.py:85
  448.3 2.1 copy-start
  455.8 8.3 slice-start
  458.6 5.5 slice-start.1
  488.3 5.5 copy-start.1
  493.8 3.4 copy-start.2
  512.6 83.8 %all-to-all-start.3 = ((bf16[2,256,4096]{2,0,1:T(2,128)(2,1)}), bf16[2,256,4096]{2,0,1:T(2,128)(2,1)}, u32[]{:S(2)}, u32[]{:S(2)}) async-start(bf16[2,256,4096]{2,0,1:T(2,128)(2,1)} %copy.25), calls=%async_computation.3 | async-start | bytes 8388608 | tf_op jit(solution)/shard_map/all_to_all | solution.py:113
  596.5 97.4 %all-to-all-start.4 = ((bf16[2,256,4096]{2,0,1:T(2,128)(2,1)}), bf16[2,256,4096]{2,0,1:T(2,128)(2,1)}, u32[]{:S(2)}, u32[]{:S(2)}) async-start(bf16[2,256,4096]{2,0,1:T(2,128)(2,1)} %copy.27), calls=%async_computation.4 | async-start | bytes 8388608 | tf_op jit(solution)/shard_map/all_to_all | solution.py:114
  616.2 216.7 %reduce-scatter.2.cloned.1.call-start = ((), (), s32[]{:S(2)}) async-start(), calls=%async_computation.7 | async-start | bytes 3145728 | tf_op jit(solution)/shard_map/reduce_scatter | solution.py:140
  715.4 68.2 %copy-start.4 = (bf16[1,256,4096]{2,1,0:T(8,128)(2,1)S(1)}, bf16[1,256,4096]{2,1,0:T(8,128)(2,1)}, u32[]{:S(2)}) copy-start(bf16[1,256,4096]{2,1,0:T(8,128)(2,1)} %copy-done.3) | copy-start | bytes 6291460
  715.4 68.2 %copy-start.5 = (f32[4096]{0:T(1024)S(1)}, f32[4096]{0:T(1024)}, u32[]{:S(2)}) copy-start(f32[4096]{0:T(1024)} %param.12) | copy-start | bytes 49156
Sparse Core Ops, SparseCore 0:
  800.5 32.2 reduce-scatter.1
where the time goes:
time: 849 us; the launch traced here: 840 us
  waiting for transfers between devices  269 us (32%)
  other arithmetic  239 us (28%)
  local copies, waits for them, and re-layouts  97.1 us (11%)
  matrix products  84.8 us (10%)
  starting transfers between devices  68.7 us (8%)
  blocking collectives  67 us (8%)
  between operations  14.1 us (2%)
    sub x16, other arithmetic, add_mode(): partial_value[1] - factor * denom_im  191 us
    all_to_all x1, waiting for transfers between devices, sequence_conv(): lax.all_to_all(section_re, 'ctx', split_axis=0, concat_axis=1, tiled=True)  71.1 us
    all_to_all x1, waiting for transfers between devices, sequence_conv(): lax.all_to_all(twist_re, 'ctx', split_axis=1, concat_axis=0, tiled=True)  69.1 us
    all_to_all x1, blocking collectives, sequence_conv(): lax.all_to_all(convolved, 'ctx', split_axis=0, concat_axis=1, tiled=True)  67 us
    all_to_all x1, waiting for transfers between devices, sequence_conv(): lax.all_to_all(twist_im, 'ctx', split_axis=1, concat_axis=0, tiled=True)  55.3 us
    all_to_all x1, waiting for transfers between devices, sequence_conv(): lax.all_to_all(product[None], 'ctx', split_axis=1, concat_axis=0, tiled=T...  40.9 us
    reduce_scatter x1, waiting for transfers between devices, on_device(): lax.psum_scatter(lax.dot_general(w_out, gated, (((0,), (1,)), ((), ())),...  32.4 us
    all_to_all x1, starting transfers between devices, sequence_conv(): lax.all_to_all(section_im, 'ctx', split_axis=0, concat_axis=1, tiled=True)  19.9 us
  transfers between devices with their start and end apart: 7, of which 5 were waited for; matrix products, arithmetic and copies ran while one was open for 30% of the time, Pallas kernels for 0%

commit v1 on v0

v1 whole, which is shorter than its diff:
```python
import functools
import math

import jax
import jax.numpy as jnp
import numpy as np
from jax import lax
from jax.experimental import pallas as pl
from jax.experimental.pallas import tpu as pltpu
from jax.sharding import PartitionSpec as P

LANES = 128
SUB = 8


def half_tables(block):
    k = np.arange(block)[:, None]
    t = np.arange(block)[None, :]
    angle = np.pi / (2 * block) * ((2 * k + 1) * t % (4 * block))
    fwd = np.concatenate([np.cos(angle), np.sin(angle)], axis=0)
    return jnp.asarray(fwd, jnp.bfloat16), jnp.asarray(fwd.T, jnp.bfloat16)


def spread(ref, modes, lanes):
    return jnp.stack(
        [jnp.broadcast_to(ref[m : m + 1, lanes], (SUB, LANES)) for m in range(modes)]
    )


def mode_weight(rates, residues, modes):
    return residues * jnp.sqrt(2.0 * rates / modes)


def local_kernel(
    proj, halo, short, rate, residue, skip, fwd, inv, query, base, state, line, taps, prod
):
    tokens, width = proj.shape[1], proj.shape[2]
    modes = rate.shape[0]
    row = lax.broadcasted_iota(jnp.int32, (1, SUB, LANES), 1).astype(jnp.float32)
    for j in range(width // LANES):
        lanes = slice(j * LANES, (j + 1) * LANES)
        feats = []
        for s in range(3):
            now = proj[s, :, lanes].astype(jnp.float32)
            line[s, SUB - 2 : SUB, :] = halo[s, :, lanes].astype(jnp.float32)
            line[s, SUB : SUB + tokens, :] = now
            mixed = (
                short[s, 0:1, lanes] * now
                + short[s, 1:2, lanes] * line[s, SUB - 1 : SUB - 1 + tokens, :]
                + short[s, 2:3, lanes] * line[s, SUB - 2 : SUB - 2 + tokens, :]
            )
            feats.append(mixed.astype(jnp.bfloat16))
        query[:, lanes] = feats[0]
        product = (feats[1].astype(jnp.float32) * feats[2].astype(jnp.float32)).astype(jnp.bfloat16)
        prod[:, lanes] = product
        line[0, SUB : SUB + tokens, :] = product.astype(jnp.float32)

        rates = spread(rate, modes, lanes)
        weight = mode_weight(rates, spread(residue, modes, lanes), modes)
        step = jnp.exp(-SUB * rates)
        power = weight * jnp.exp(-rates * row)

        def advance(i, carry):
            power, held = carry
            rows = []
            for half in range(2):
                start = pl.multiple_of(SUB + i * 2 * SUB + half * SUB, SUB)
                held = held * step + line[0, pl.ds(start, SUB), :][None]
                rows.append(jnp.sum(power, axis=0))
                power = power * step
            at = pl.multiple_of(i * 2 * SUB, 2 * SUB)
            taps[pl.ds(at, 2 * SUB), lanes] = jnp.concatenate(rows, axis=0).astype(jnp.bfloat16)
            return power, held

        _, held = lax.fori_loop(
            0, tokens // (2 * SUB), advance, (power, jnp.zeros_like(power))
        )
        held = held * jnp.exp(-rates * (SUB - 1 - row))
        state[:, lanes] = jnp.sum(held, axis=1).astype(state.dtype)

    sig = jnp.dot(fwd[...], prod[...], preferred_element_type=jnp.float32)
    fil = jnp.dot(fwd[...], taps[...], preferred_element_type=jnp.float32)
    cs, ss, cf, sf = sig[:tokens], sig[tokens:], fil[:tokens], fil[tokens:]
    both = jnp.concatenate(
        [(cs * cf - ss * sf).astype(jnp.bfloat16), (cs * sf + ss * cf).astype(jnp.bfloat16)], axis=0
    )
    conv = jnp.dot(inv[...], both, preferred_element_type=jnp.float32) * (1.0 / tokens)
    base[...] = conv + skip[...] * prod[...].astype(jnp.float32)


def gate_kernel(query, base, enter, rate, residue, w_out, out, gated):
    tokens, channels = query.shape
    modes = rate.shape[0]

    @pl.when(pl.program_id(0) == 0)
    def _():
        row = lax.broadcasted_iota(jnp.int32, (1, SUB, LANES), 1).astype(jnp.float32)

        @pl.loop(0, channels // LANES)
        def _(j):
            lanes = pl.ds(pl.multiple_of(j * LANES, LANES), LANES)
            rates = spread(rate, modes, lanes)
            weight = mode_weight(rates, spread(residue, modes, lanes), modes)
            step = jnp.exp(-SUB * rates)
            power = weight * jnp.exp(-rates * (row + 1.0)) * spread(enter, modes, lanes)

            def advance(i, power):
                rows = []
                for half in range(2):
                    rows.append(jnp.sum(power, axis=0))
                    power = power * step
                at = pl.ds(pl.multiple_of(i * 2 * SUB, 2 * SUB), 2 * SUB)
                total = jnp.concatenate(rows, axis=0) + base[at, lanes]
                gated[at, lanes] = (query[at, lanes].astype(jnp.float32) * total).astype(
                    jnp.bfloat16
                )
                return power

            lax.fori_loop(0, tokens // (2 * SUB), advance, power)

    out[0] = jnp.dot(
        gated[...], w_out[...], preferred_element_type=jnp.float32
    ).astype(jnp.bfloat16)


def on_device(projected, short_weight, rate, residue, skip, w_out):
    count = lax.axis_size("ctx")
    parts = lax.axis_size("tp")
    rank = lax.axis_index("ctx")
    _, tokens, channels = projected.shape
    modes = rate.shape[1]
    outputs = w_out.shape[1]
    rate_t, residue_t = rate.T, residue.T
    halo = lax.ppermute(
        projected[:, -2:, :], "ctx", [(i, i + 1) for i in range(count - 1)]
    )
    fwd, inv = half_tables(tokens)
    width = min(512, channels)
    by_col = lambda *lead: pl.BlockSpec(lead + (width,), lambda i: (0,) * len(lead) + (i,))
    whole = lambda shape: pl.BlockSpec(shape, lambda i: (0,) * len(shape))
    query, base, state = pl.pallas_call(
        local_kernel,
        grid=(channels // width,),
        in_specs=[
            by_col(3, tokens), by_col(3, 2), by_col(3, 3), by_col(modes), by_col(modes),
            by_col(1), whole(fwd.shape), whole(inv.shape),
        ],
        out_specs=[by_col(tokens), by_col(tokens), by_col(modes)],
        out_shape=[
            jax.ShapeDtypeStruct((tokens, channels), jnp.bfloat16),
            jax.ShapeDtypeStruct((tokens, channels), jnp.float32),
            jax.ShapeDtypeStruct((modes, channels), jnp.float32),
        ],
        scratch_shapes=[
            pltpu.VMEM((3, tokens + SUB, LANES), jnp.float32),
            pltpu.VMEM((tokens, width), jnp.bfloat16),
            pltpu.VMEM((tokens, width), jnp.bfloat16),
        ],
        compiler_params=pltpu.CompilerParams(vmem_limit_bytes=40 * 2**20),
        name="local",
    )(projected, halo, short_weight, rate_t, residue_t, skip[None], fwd, inv)

    share = channels // count
    got = lax.all_to_all(
        state.astype(jnp.bfloat16).reshape(modes, count, share).transpose(1, 0, 2),
        "ctx", split_axis=0, concat_axis=0, tiled=True,
    ).astype(jnp.float32)
    decay = jnp.exp(-float(tokens) * lax.dynamic_slice_in_dim(rate_t, rank * share, share, 1))
    held = jnp.zeros((modes, share), jnp.float32)
    enter = []
    for i in range(count):
        enter.append(held)
        held = held * decay + got[i]
    enter = lax.all_to_all(
        jnp.stack(enter).astype(jnp.bfloat16), "ctx", split_axis=0, concat_axis=0, tiled=True
    )
    enter = enter.transpose(1, 0, 2).reshape(modes, channels).astype(jnp.float32)

    tile = min(512, outputs // parts)
    per = outputs // parts // tile
    summed = pl.pallas_call(
        gate_kernel,
        grid=(outputs // tile,),
        in_specs=[
            whole(query.shape), whole(base.shape), whole(enter.shape), whole(rate_t.shape),
            whole(rate_t.shape), pl.BlockSpec((channels, tile), lambda i: (0, i)),
        ],
        out_specs=pl.BlockSpec((1, tokens, tile), lambda i: (i // per, 0, i % per)),
        out_shape=jax.ShapeDtypeStruct((parts, tokens, outputs // parts), jnp.bfloat16),
        scratch_shapes=[pltpu.VMEM((tokens, channels), jnp.bfloat16)],
        compiler_params=pltpu.CompilerParams(vmem_limit_bytes=50 * 2**20),
        name="gate",
    )(query, base, enter, rate_t, residue_t, w_out)
    return lax.psum_scatter(summed, "tp", scatter_dimension=0, tiled=True)[0]


def solution(mesh):
    return jax.shard_map(
        on_device,
        mesh=mesh,
        in_specs=(
            P(None, "ctx", "tp"),
            P(None, None, "tp"),
            P("tp", None),
            P("tp", None),
            P("tp"),
            P("tp", None),
        ),
        out_specs=P("ctx", "tp"),
        check_vma=False,
    )
```

time: 849 us -> 150 us (0.18)
  other arithmetic: 239 us -> 0.39 us
  waiting for transfers between devices: 269 us -> 38.4 us
  matrix products: 84.8 us -> 0 us
  local copies, waits for them, and re-layouts: 97.1 us -> 13.2 us
  Pallas kernels: 0 us -> 61 us
  starting transfers between devices: 68.7 us -> 11.9 us
  blocking collectives: 67 us -> 10.5 us
    all_to_all x5 -> x1, waiting for transfers between devices: 236 us -> 7.87 us  [on_device(): lax.all_to_all(state.astype(jnp.bfloat16).reshape(modes, count, share).tr...]
    sub x16 -> x0, other arithmetic: 191 us -> none  [add_mode(): partial_value[1] - factor * denom_im]
    dot_general x13 -> x0, matrix products: 84.8 us -> none  [the longest x1 16.7 us: on_device(): lax.dot_general(w_out, gated, (((0,), (1,)), ((), ())), preferred_element...]
    pallas_call x0 -> x2, Pallas kernels: none -> 61 us  [the longest x1 31.3 us: on_device(): pl.pallas_call(gate_kernel, grid=(outputs // tile,), in_specs=[whole(quer...]
    all_to_all x5 -> x1, starting transfers between devices: 66.1 us -> 9.53 us  [on_device(): lax.all_to_all(state.astype(jnp.bfloat16).reshape(modes, count, share).tr...]
    all_to_all x1, blocking collectives: 67 us -> 10.5 us  [on_device(): lax.all_to_all(jnp.stack(enter).astype(jnp.bfloat16), 'ctx', split_axis=0...]
    all_to_all x6 -> x0, local copies, waits for them, and re-layouts: 39.8 us -> none  [the longest x2 17.3 us: sequence_conv(): lax.all_to_all(twist_im, 'ctx', split_axis=1, concat_axis=0, tiled=True)]
    convert_element_type x6 -> x1, local copies, waits for them, and re-layouts: 35.8 us -> 0.02 us  [on_device(): enter.transpose(1, 0, 2).reshape(modes, channels).astype(jnp.float32)]
  transfers between devices with their start and end apart: 7 -> 3, of which waited for: 5 -> 3; matrix products, arithmetic and copies ran while one was open for 30% -> 0% of each run, Pallas kernels for 0% -> 0%
where the time goes in v1:
time: 150 us; the launch traced here: 149 us
  Pallas kernels  61 us (41%)
  waiting for transfers between devices  38.4 us (26%)
  between operations  13.6 us (9%)
  local copies, waits for them, and re-layouts  13.2 us (9%)
  starting transfers between devices  11.9 us (8%)
  blocking collectives  10.5 us (7%)
    pallas_call x1, Pallas kernels, on_device(): pl.pallas_call(gate_kernel, grid=(outputs // tile,), in_specs=[whole(quer...  31.3 us
    pallas_call x1, Pallas kernels, on_device(): pl.pallas_call(local_kernel, grid=(channels // width,), in_specs=[by_col(...  29.8 us
    reduce_scatter x1, waiting for transfers between devices, on_device(): return lax.psum_scatter(summed, 'tp', scatter_dimension=0, tiled=True)[0]  29.7 us
    unnamed x23, local copies, waits for them, and re-layouts  11.5 us
    all_to_all x1, blocking collectives, on_device(): lax.all_to_all(jnp.stack(enter).astype(jnp.bfloat16), 'ctx', split_axis=0...  10.5 us
    all_to_all x1, starting transfers between devices, on_device(): lax.all_to_all(state.astype(jnp.bfloat16).reshape(modes, count, share).tr...  9.53 us
    all_to_all x1, waiting for transfers between devices, on_device(): lax.all_to_all(state.astype(jnp.bfloat16).reshape(modes, count, share).tr...  7.87 us
  transfers between devices with their start and end apart: 3, of which 3 were waited for; matrix products, arithmetic and copies ran while one was open for 0% of the time, Pallas kernels for 0%

profile of v1, /device:TPU:0, one launch (start us, length us, event | category | flops | bytes accessed | tf_op | source)
XLA Modules:
  0.0 149.1 jit_solution(8752686624773709717)
XLA Ops:
  6.5 1.0 slice.48
  7.5 2.4 %collective-permute-start = (bf16[3,2,4096]{2,1,0:T(2,128)(2,1)S(1)}, bf16[3,2,4096]{2,1,0:T(2,128)(2,1)S(1)}, u32[]{:S(2)}, u32[]{:S(2)}) collective-permute-start(bf16[3,2,4096]{2,1,0:T(2,128)(2,1)S(1)} %slice.48), channel_id=1, source_target_pairs={{0,2},{2,4},{4,6},{6,8},{8,10},{10,12},{12,14},{14,16},{16,18},{18... | collective-permute-start | bytes 147464 | tf_op jit(solution)/shard_map/ppermute | solution.py:134
  9.9 0.9 collective-permute-done.halo
  10.7 0.0 copy-start
  10.7 2.8 %copy-done = bf16[3,256,4096]{2,1,0:T(8,128)(2,1)S(1)} copy-done((bf16[3,256,4096]{2,1,0:T(8,128)(2,1)S(1)}, bf16[3,256,4096]{2,1,0:T(8,128)(2,1)}, u32[]{:S(2)}) %copy-start) | copy-done | bytes 6291480
  13.5 0.0 copy-start.2
  13.5 0.9 copy-done.2
  14.5 0.0 copy-start.5
  14.5 0.9 copy-done.5
  15.4 0.9 copy-done.7
  16.4 0.0 copy-start.8
  16.4 0.9 copy-done.8
  17.3 0.0 copy-start.9
  17.3 0.9 copy-done.9
  18.3 0.0 copy-start.10
  18.3 0.7 copy-done.10
  19.0 0.0 copy-start.3
  19.0 0.0 copy-start.6
  19.0 29.8 %local.1 = (bf16[256,4096]{1,0:T(8,128)(2,1)S(1)}, f32[256,4096]{1,0:T(8,128)S(1)}, f32[16,4096]{1,0:T(8,128)S(1)}) custom-call(bf16[3,256,4096]{2,1,0:T(8,128)(2,1)S(1)} %copy-done, bf16[3,2,4096]{2,1,0:T(2,128)(2,1)S(1)} %collective-permute-done.halo, f32[3,3,4096]{2,1,0:T(4,128)S(1)} %copy-done.9, f32[16,4096]{1,0:T(8,128)S(1)} %bitcast.276, ...), custom_call_target="tpu_custom_call" | custom-call | tf_op jit(solution)/shard_map/local/pallas_call | solution.py:141
  48.8 0.0 copy-start.1
  48.8 1.9 %copy-done.1 = f32[256,4096]{1,0:T(8,128)} copy-done((f32[256,4096]{1,0:T(8,128)}, f32[256,4096]{1,0:T(8,128)S(1)}, u32[]{:S(2)}) %copy-start.1) | copy-done | bytes 4194328
  50.7 1.4 copy-done.4
  52.1 0.7 copy.14
  52.8 9.5 %all-to-all-start = ((bf16[16,16,256]{2,1,0:T(8,128)(2,1)}), bf16[16,16,256]{2,1,0:T(8,128)(2,1)S(1)}, u32[]{:S(2)}, u32[]{:S(2)}) async-start(bf16[16,16,256]{2,1,0:T(8,128)(2,1)} %bitcast.275), calls=%async_computation | async-start | bytes 262144 | tf_op jit(solution)/shard_map/all_to_all | solution.py:164
  62.3 0.0 reduce-scatter.2.cloned.1.call-start
  62.4 7.9 %all-to-all-done = bf16[16,16,256]{2,1,0:T(8,128)(2,1)S(1)} async-done(((bf16[16,16,256]{2,1,0:T(8,128)(2,1)}), bf16[16,16,256]{2,1,0:T(8,128)(2,1)S(1)}, u32[]{:S(2)}, u32[]{:S(2)}) %all-to-all-start) | async-done | bytes 131104 | tf_op jit(solution)/shard_map/all_to_all | solution.py:164
  70.3 0.0 copy-done.3
  70.7 10.5 %all_to_all.10 = bf16[16,16,256]{2,1,0:T(8,128)(2,1)S(1)} all-to-all(bf16[16,16,256]{2,1,0:T(8,128)(2,1)S(1)} %constant_dynamic-update-slice_fusion), channel_id=1, replica_groups=mesh['ctx'=16,'tp'=2] {'ctx'}, dimensions={0} | all-to-all | bytes 262144 | tf_op jit(solution)/shard_map/all_to_all | solution.py:174
  81.3 0.0 copy-done.6
  81.3 31.3 %gate.1 = bf16[2,256,2048]{2,1,0:T(8,128)(2,1)} custom-call(bf16[256,4096]{1,0:T(8,128)(2,1)} %copy-done.4, f32[256,4096]{1,0:T(8,128)} %copy-done.1, f32[16,4096]{1,0:T(8,128)S(1)} %bitcast.278, f32[16,4096]{1,0:T(8,128)S(1)} %bitcast.277, f32[16,4096]{1,0:T(8,128)S(1)} %bitcast.280, bf16[4096,4096]{1,0:T(8,128)(2,1)} %w_out.1), custom_call_target="tpu_custom_call" | custom-call | tf_op jit(solution)/shard_map/gate/pallas_call | solution.py:181
  112.6 0.0 reduce-scatter.2.cloned.1.call-update
  112.6 29.7 %reduce-scatter.2.cloned.1.call-done = bf16[1,256,2048]{2,1,0:T(8,128)(2,1)} async-done(((bf16[2,256,2048]{2,1,0:T(8,128)(2,1)}), bf16[1,256,2048]{2,1,0:T(8,128)(2,1)}) %reduce-scatter.2.cloned.1.call-update) | async-done | bytes 1048592 | tf_op jit(solution)/shard_map/reduce_scatter | solution.py:194
  (22 shorter events, 0.4 us)
Async XLA Ops:
  7.5 3.2 %collective-permute-start = (bf16[3,2,4096]{2,1,0:T(2,128)(2,1)S(1)}, bf16[3,2,4096]{2,1,0:T(2,128)(2,1)S(1)}, u32[]{:S(2)}, u32[]{:S(2)}) collective-permute-start(bf16[3,2,4096]{2,1,0:T(2,128)(2,1)S(1)} %slice.48), channel_id=1, source_target_pairs={{0,2},{2,4},{4,6},{6,8},{8,10},{10,12},{12,14},{14,16},{16,18},{18... | collective-permute-start | bytes 147464 | tf_op jit(solution)/shard_map/ppermute | solution.py:134
  10.7 2.8 %copy-start = (bf16[3,256,4096]{2,1,0:T(8,128)(2,1)S(1)}, bf16[3,256,4096]{2,1,0:T(8,128)(2,1)}, u32[]{:S(2)}) copy-start(bf16[3,256,4096]{2,1,0:T(8,128)(2,1)} %proj.1) | copy-start | bytes 18874372
  13.5 0.9 copy-start.2
  14.5 0.9 copy-start.5
  15.4 0.9 copy-start.7
  16.4 0.9 copy-start.8
  17.3 0.9 copy-start.9
  18.3 0.7 copy-start.10
  19.0 51.3 %copy-start.3 = (f32[4096,16]{0,1:T(8,128)S(1)}, f32[4096,16]{0,1:T(8,128)}, u32[]{:S(2)}) copy-start(f32[4096,16]{0,1:T(8,128)} %param.10) | copy-start | bytes 786436
  19.0 62.3 %copy-start.6 = (f32[4096,16]{0,1:T(8,128)S(1)}, f32[4096,16]{0,1:T(8,128)}, u32[]{:S(2)}) copy-start(f32[4096,16]{0,1:T(8,128)} %param.11) | copy-start | bytes 786436
  48.8 1.9 %copy-start.1 = (f32[256,4096]{1,0:T(8,128)}, f32[256,4096]{1,0:T(8,128)S(1)}, u32[]{:S(2)}) copy-start(f32[256,4096]{1,0:T(8,128)S(1)} %get-tuple-element.9.base) | copy-start | bytes 12582916
  50.7 1.4 copy-start.4
  52.8 17.5 %all-to-all-start = ((bf16[16,16,256]{2,1,0:T(8,128)(2,1)}), bf16[16,16,256]{2,1,0:T(8,128)(2,1)S(1)}, u32[]{:S(2)}, u32[]{:S(2)}) async-start(bf16[16,16,256]{2,1,0:T(8,128)(2,1)} %bitcast.275), calls=%async_computation | async-start | bytes 262144 | tf_op jit(solution)/shard_map/all_to_all | solution.py:164
  62.3 80.0 %reduce-scatter.2.cloned.1.call-start = ((), (), s32[]{:S(2)}) async-start(), calls=%async_computation.3 | async-start | bytes 3145728 | tf_op jit(solution)/shard_map/reduce_scatter | solution.py:194
Sparse Core Ops, SparseCore 0:
  112.7 29.5 reduce-scatter.1

commit v2 on v1

v2 whole, which is shorter than its diff:
```python
import functools
import math

import jax
import jax.numpy as jnp
import numpy as np
from jax import lax
from jax.experimental import pallas as pl
from jax.experimental.pallas import tpu as pltpu
from jax.sharding import PartitionSpec as P

LANES = 128
SUB = 8
MESH = pl.DeviceIdType.MESH


def half_tables(block):
    k = np.arange(block)[:, None]
    t = np.arange(block)[None, :]
    angle = np.pi / (2 * block) * ((2 * k + 1) * t % (4 * block))
    fwd = np.concatenate([np.cos(angle), np.sin(angle)], axis=0)
    return jnp.asarray(fwd, jnp.bfloat16), jnp.asarray(fwd.T, jnp.bfloat16)


def spread(rows):
    return jnp.stack(
        [jnp.broadcast_to(rows[m : m + 1], (SUB, LANES)) for m in range(rows.shape[0])]
    )


def mode_weight(rates, residues, modes):
    return residues * jnp.sqrt(2.0 * rates / modes)


def local_kernel(
    proj, halo, short, rate, residue, skip, fwd, inv, query, base, state, line, taps, prod
):
    tokens, width = proj.shape[1], proj.shape[2]
    modes = rate.shape[1]
    row = lax.broadcasted_iota(jnp.int32, (1, SUB, LANES), 1).astype(jnp.float32)
    for j in range(width // LANES):
        lanes = slice(j * LANES, (j + 1) * LANES)
        feats = []
        for s in range(3):
            now = proj[s, :, lanes].astype(jnp.float32)
            line[s, SUB - 2 : SUB, :] = halo[s, :, lanes].astype(jnp.float32)
            line[s, SUB : SUB + tokens, :] = now
            mixed = (
                short[s, 0:1, lanes] * now
                + short[s, 1:2, lanes] * line[s, SUB - 1 : SUB - 1 + tokens, :]
                + short[s, 2:3, lanes] * line[s, SUB - 2 : SUB - 2 + tokens, :]
            )
            feats.append(mixed.astype(jnp.bfloat16))
        query[:, lanes] = feats[0]
        product = (feats[1].astype(jnp.float32) * feats[2].astype(jnp.float32)).astype(jnp.bfloat16)
        prod[:, lanes] = product
        line[0, SUB : SUB + tokens, :] = product.astype(jnp.float32)

        rates = spread(rate[j])
        weight = mode_weight(rates, spread(residue[j]), modes)
        step = jnp.exp(-SUB * rates)
        power = weight * jnp.exp(-rates * row)

        def advance(i, carry):
            power, held = carry
            rows = []
            for half in range(2):
                start = pl.multiple_of(SUB + i * 2 * SUB + half * SUB, SUB)
                held = held * step + line[0, pl.ds(start, SUB), :][None]
                rows.append(jnp.sum(power, axis=0))
                power = power * step
            at = pl.multiple_of(i * 2 * SUB, 2 * SUB)
            taps[pl.ds(at, 2 * SUB), lanes] = jnp.concatenate(rows, axis=0).astype(jnp.bfloat16)
            return power, held

        _, held = lax.fori_loop(
            0, tokens // (2 * SUB), advance, (power, jnp.zeros_like(power))
        )
        held = held * jnp.exp(-rates * (SUB - 1 - row))
        state[j] = jnp.sum(held, axis=1).astype(state.dtype)

    sig = jnp.dot(fwd[...], prod[...], preferred_element_type=jnp.float32)
    fil = jnp.dot(fwd[...], taps[...], preferred_element_type=jnp.float32)
    cs, ss, cf, sf = sig[:tokens], sig[tokens:], fil[:tokens], fil[tokens:]
    both = jnp.concatenate(
        [(cs * cf - ss * sf).astype(jnp.bfloat16), (cs * sf + ss * cf).astype(jnp.bfloat16)], axis=0
    )
    conv = jnp.dot(inv[...], both, preferred_element_type=jnp.float32) * (1.0 / tokens)
    base[...] = conv + skip[...] * prod[...].astype(jnp.float32)


def finish_kernel(
    state, query, base, rate, residue, decay_rate, w_out, out,
    w_buf, gated, got, enter_out, enter, send, recv, own,
    w_sem, s1, r1, s2, r2, s3, r3,
):
    tokens, channels = query.shape
    modes = rate.shape[1]
    count, share = state.shape[0], state.shape[1]
    parts, rank = lax.axis_size("tp"), lax.axis_index("ctx")
    me = lax.axis_index("tp")
    tiles, _, tile = w_buf.shape
    per = tiles // parts
    away = tiles - per

    def load(i):
        peer = lax.rem(me + 1 + i // per, parts)
        col = pl.multiple_of((peer * per + i % per) * tile, tile)
        return pltpu.make_async_copy(w_out.at[:, pl.ds(col, tile)], w_buf.at[i], w_sem.at[i])

    @pl.loop(0, tiles)
    def _(i):
        load(i).start()

    barrier = pltpu.get_barrier_semaphore()

    @pl.loop(1, count)
    def _(o):
        pl.semaphore_signal(
            barrier, inc=1, device_id=(lax.rem(rank + o, count), me), device_id_type=MESH
        )

    @pl.loop(1, parts)
    def _(o):
        pl.semaphore_signal(
            barrier, inc=1, device_id=(rank, lax.rem(me + o, parts)), device_id_type=MESH
        )

    pl.semaphore_wait(barrier, count + parts - 2)

    def hop(src, dst, peer, slot, sent, landed):
        return pltpu.make_async_remote_copy(
            src_ref=src.at[peer], dst_ref=dst.at[slot], send_sem=sent.at[peer],
            recv_sem=landed.at[slot], device_id=(peer, me), device_id_type=MESH,
        )

    @pl.loop(1, count)
    def _(o):
        hop(state, got, lax.rem(rank + o, count), rank, s1, r1).start()

    got[rank] = state[rank]

    @pl.loop(1, count)
    def _(o):
        peer = lax.rem(rank + o, count)
        hop(state, got, peer, peer, s1, r1).wait()

    decay = jnp.exp(-float(tokens) * decay_rate[rank])

    def prefix(i, held):
        enter_out[i] = held.astype(enter_out.dtype)
        return held * decay + got[i].astype(jnp.float32)

    lax.fori_loop(0, count, prefix, jnp.zeros((share, LANES), jnp.float32))

    @pl.loop(1, count)
    def _(o):
        hop(enter_out, enter, lax.rem(rank + o, count), rank, s2, r2).start()

    enter[rank] = enter_out[rank]

    @pl.loop(1, count)
    def _(o):
        peer = lax.rem(rank + o, count)
        hop(enter_out, enter, peer, peer, s2, r2).wait()

    row = lax.broadcasted_iota(jnp.int32, (1, SUB, LANES), 1).astype(jnp.float32)

    def entering(j):
        if share >= modes:
            fold = share // modes
            at = pl.multiple_of((j % fold) * modes, modes)
            return spread(enter[j // fold, pl.ds(at, modes), :].astype(jnp.float32))
        fold = modes // share
        return jnp.concatenate(
            [spread(enter[j * fold + i].astype(jnp.float32)) for i in range(fold)], axis=0
        )

    @pl.loop(0, channels // LANES)
    def _(j):
        lanes = pl.ds(pl.multiple_of(j * LANES, LANES), LANES)
        rates = spread(rate[j])
        weight = mode_weight(rates, spread(residue[j]), modes)
        step = jnp.exp(-SUB * rates)
        power = weight * jnp.exp(-rates * (row + 1.0)) * entering(j)

        def advance(i, power):
            rows = []
            for half in range(2):
                rows.append(jnp.sum(power, axis=0))
                power = power * step
            at = pl.ds(pl.multiple_of(i * 2 * SUB, 2 * SUB), 2 * SUB)
            total = jnp.concatenate(rows, axis=0) + base[at, lanes]
            gated[at, lanes] = (query[at, lanes].astype(jnp.float32) * total).astype(jnp.bfloat16)
            return power

        lax.fori_loop(0, tokens // (2 * SUB), advance, power)

    def product(i):
        load(i).wait()
        return jnp.dot(gated[...], w_buf[i], preferred_element_type=jnp.float32)

    def give(i):
        peer = lax.rem(me + 1 + i // per, parts)
        return pltpu.make_async_remote_copy(
            src_ref=send.at[i], dst_ref=recv.at[i], send_sem=s3.at[i], recv_sem=r3.at[i],
            device_id=(rank, peer), device_id_type=MESH,
        )

    @pl.loop(0, away)
    def _(i):
        send[i] = product(i).astype(jnp.bfloat16)
        give(i).start()

    @pl.loop(0, per)
    def _(t):
        own[t] = product(away + t)

    for t in range(per):
        total = own[t]
        for o in range(parts - 1):
            give(o * per + t).wait()
            total = total + recv[o * per + t].astype(jnp.float32)
        out[:, t * tile : (t + 1) * tile] = total.astype(out.dtype)


def on_device(projected, short_weight, rate, residue, skip, w_out):
    count = lax.axis_size("ctx")
    parts = lax.axis_size("tp")
    _, tokens, channels = projected.shape
    modes = rate.shape[1]
    outputs = w_out.shape[1]
    blocks = channels // LANES
    rate_b = rate.reshape(blocks, LANES, modes).transpose(0, 2, 1)
    residue_b = residue.reshape(blocks, LANES, modes).transpose(0, 2, 1)
    halo = lax.ppermute(
        projected[:, -2:, :], "ctx", [(i, i + 1) for i in range(count - 1)]
    )
    fwd, inv = half_tables(tokens)
    width = min(512, channels)
    by_col = lambda *lead: pl.BlockSpec(lead + (width,), lambda i: (0,) * len(lead) + (i,))
    by_block = pl.BlockSpec((width // LANES, modes, LANES), lambda i: (i, 0, 0))
    whole = lambda shape: pl.BlockSpec(shape, lambda i: (0,) * len(shape))
    query, base, state = pl.pallas_call(
        local_kernel,
        grid=(channels // width,),
        in_specs=[
            by_col(3, tokens), by_col(3, 2), by_col(3, 3), by_block, by_block,
            by_col(1), whole(fwd.shape), whole(inv.shape),
        ],
        out_specs=[by_col(tokens), by_col(tokens), by_block],
        out_shape=[
            jax.ShapeDtypeStruct((tokens, channels), jnp.bfloat16),
            jax.ShapeDtypeStruct((tokens, channels), jnp.float32),
            jax.ShapeDtypeStruct((blocks, modes, LANES), jnp.bfloat16),
        ],
        scratch_shapes=[
            pltpu.VMEM((3, tokens + SUB, LANES), jnp.float32),
            pltpu.VMEM((tokens, width), jnp.bfloat16),
            pltpu.VMEM((tokens, width), jnp.bfloat16),
        ],
        compiler_params=pltpu.CompilerParams(vmem_limit_bytes=40 * 2**20),
        name="local",
    )(projected, halo, short_weight, rate_b, residue_b, skip[None], fwd, inv)

    share = blocks * modes // count
    each = outputs // parts
    tile = min(512, each)
    tiles = outputs // tile
    away = tiles - each // tile
    vmem = pl.BlockSpec(memory_space=pltpu.VMEM)
    return pl.pallas_call(
        finish_kernel,
        in_specs=[vmem] * 6 + [pl.BlockSpec(memory_space=pl.ANY)],
        out_specs=vmem,
        out_shape=jax.ShapeDtypeStruct((tokens, each), jnp.bfloat16),
        scratch_shapes=[
            pltpu.VMEM((tiles, channels, tile), jnp.bfloat16),
            pltpu.VMEM((tokens, channels), jnp.bfloat16),
            pltpu.VMEM((count, share, LANES), jnp.bfloat16),
            pltpu.VMEM((count, share, LANES), jnp.bfloat16),
            pltpu.VMEM((count, share, LANES), jnp.bfloat16),
            pltpu.VMEM((away, tokens, tile), jnp.bfloat16),
            pltpu.VMEM((away, tokens, tile), jnp.bfloat16),
            pltpu.VMEM((each // tile, tokens, tile), jnp.float32),
            pltpu.SemaphoreType.DMA((tiles,)),
        ]
        + [pltpu.SemaphoreType.DMA((count,))] * 4
        + [pltpu.SemaphoreType.DMA((away,))] * 2,
        compiler_params=pltpu.CompilerParams(
            vmem_limit_bytes=56 * 2**20, collective_id=0, has_side_effects=True
        ),
        name="finish",
    )(
        state.reshape(count, share, LANES), query, base, rate_b, residue_b,
        rate_b.reshape(count, share, LANES), w_out,
    )


def solution(mesh):
    return jax.shard_map(
        on_device,
        mesh=mesh,
        in_specs=(
            P(None, "ctx", "tp"),
            P(None, None, "tp"),
            P("tp", None),
            P("tp", None),
            P("tp"),
            P("tp", None),
        ),
        out_specs=P("ctx", "tp"),
        check_vma=False,
    )
```

time: 150 us -> 108 us (0.72)
  waiting for transfers between devices: 38.4 us -> 0.01 us
  Pallas kernels: 61 us -> 90.1 us
  between operations: 13.6 us -> 0.06 us
  blocking collectives: 10.5 us -> 0 us
  starting transfers between devices: 11.9 us -> 2.36 us
  local copies, waits for them, and re-layouts: 13.2 us -> 15.5 us
    reduce_scatter x1 -> x0, waiting for transfers between devices: 29.7 us -> none  [on_device(): return lax.psum_scatter(summed, 'tp', scatter_dimension=0, tiled=True)[0]]
    pallas_call x1, Pallas kernels: 31.3 us -> 60.3 us  [on_device(): pl.pallas_call(finish_kernel, in_specs=[vmem] * 6 + [pl.BlockSpec(memory_...]
    all_to_all x1 -> x0, blocking collectives: 10.5 us -> none  [on_device(): lax.all_to_all(jnp.stack(enter).astype(jnp.bfloat16), 'ctx', split_axis=0...]
    all_to_all x1 -> x0, starting transfers between devices: 9.53 us -> none  [on_device(): lax.all_to_all(state.astype(jnp.bfloat16).reshape(modes, count, share).tr...]
    all_to_all x1 -> x0, waiting for transfers between devices: 7.87 us -> none  [on_device(): lax.all_to_all(state.astype(jnp.bfloat16).reshape(modes, count, share).tr...]
  transfers between devices with their start and end apart: 3 -> 1, of which waited for: 3 -> 0; matrix products, arithmetic and copies ran while one was open for 0% -> 2% of each run, Pallas kernels for 0% -> 0%
where the time goes in v2:
time: 108 us
  Pallas kernels  90.1 us (83%)
  local copies, waits for them, and re-layouts  15.5 us (14%)
  starting transfers between devices  2.36 us (2%)
    pallas_call x1, Pallas kernels, on_device(): pl.pallas_call(finish_kernel, in_specs=[vmem] * 6 + [pl.BlockSpec(memory_...  60.3 us
    pallas_call x1, Pallas kernels, on_device(): pl.pallas_call(local_kernel, grid=(channels // width,), in_specs=[by_col(...  29.9 us
    unnamed x23, local copies, waits for them, and re-layouts  12.7 us
    ppermute x1, starting transfers between devices, on_device(): lax.ppermute(projected[:, -2:, :], 'ctx', [(i, i + 1) for i in range(coun...  2.36 us
  transfers between devices with their start and end apart: 1, of which 0 were waited for; matrix products, arithmetic and copies ran while one was open for 2% of the time, Pallas kernels for 0%

profile of v2, /device:TPU:0, one launch (start us, length us, event | category | flops | bytes accessed | tf_op | source)
XLA Modules:
  0.0 108.1 jit_solution(12881868095431446924)
XLA Ops:
  0.0 0.0 copy-start
  0.0 1.0 slice.3
  1.0 2.4 %collective-permute-start = (bf16[3,2,4096]{2,1,0:T(2,128)(2,1)S(1)}, bf16[3,2,4096]{2,1,0:T(2,128)(2,1)S(1)}, u32[]{:S(2)}, u32[]{:S(2)}) collective-permute-start(bf16[3,2,4096]{2,1,0:T(2,128)(2,1)S(1)} %slice.3), channel_id=1, source_target_pairs={{0,2},{2,4},{4,6},{6,8},{8,10},{10,12},{12,14},{14,16},{16,18},{18... | collective-permute-start | bytes 147464 | tf_op jit(solution)/shard_map/ppermute | solution.py:236
  3.4 0.0 copy-done
  3.4 1.7 %copy_bitcast_fusion = (f32[32,128,16]{1,2,0:T(8,128)}, f32[32,16,128]{2,1,0:T(8,128)S(1)}, f32[32,16,128]{2,1,0:T(8,128)S(1)}) fusion(f32[4096,16]{0,1:T(8,128)S(1)} %copy-done, f32[4096,16]{0,1:T(8,128)} %param.10), kind=kLoop, calls=%fused_computation.1 | loop fusion | bytes 1310720 | tf_op jit(solution)/shard_map/reshape | solution.py:234
  5.1 0.0 copy-start.3
  5.1 0.0 copy-start.4
  5.1 0.0 collective-permute-done.halo
  5.1 0.0 copy-start.1
  5.1 3.0 %copy-done.1 = bf16[3,256,4096]{2,1,0:T(8,128)(2,1)S(1)} copy-done((bf16[3,256,4096]{2,1,0:T(8,128)(2,1)S(1)}, bf16[3,256,4096]{2,1,0:T(8,128)(2,1)}, u32[]{:S(2)}) %copy-start.1) | copy-done | bytes 6291480
  8.1 0.0 copy-start.6
  8.1 0.9 copy-done.6
  9.1 0.0 copy-start.7
  9.1 0.9 copy-done.7
  10.0 0.0 copy-start.8
  10.0 0.9 copy-done.8
  10.9 0.0 copy-start.10
  10.9 0.7 copy-done.10
  11.7 29.9 %local.1 = (bf16[256,4096]{1,0:T(8,128)(2,1)S(1)}, f32[256,4096]{1,0:T(8,128)S(1)}, bf16[32,16,128]{2,1,0:T(8,128)(2,1)S(1)}) custom-call(bf16[3,256,4096]{2,1,0:T(8,128)(2,1)S(1)} %copy-done.1, bf16[3,2,4096]{2,1,0:T(2,128)(2,1)S(1)} %collective-permute-done.halo, f32[3,3,4096]{2,1,0:T(4,128)S(1)} %copy-done.8, f32[32,16,128]{2,1,0:T(8,128)S(1)} %get-tuple-element.12.rate, ...), custom_call_target="tpu_custom_call" | custom-call | tf_op jit(solution)/shard_map/local/pallas_call | solution.py:244
  41.5 0.0 copy-start.2
  41.6 1.9 %copy-done.2 = f32[256,4096]{1,0:T(8,128)} copy-done((f32[256,4096]{1,0:T(8,128)}, f32[256,4096]{1,0:T(8,128)S(1)}, u32[]{:S(2)}) %copy-start.2) | copy-done | bytes 4194328
  43.5 0.0 copy-start.5
  43.5 1.3 %copy-done.5 = bf16[256,4096]{1,0:T(8,128)(2,1)} copy-done((bf16[256,4096]{1,0:T(8,128)(2,1)}, bf16[256,4096]{1,0:T(8,128)(2,1)S(1)}, u32[]{:S(2)}) %copy-start.5) | copy-done | bytes 2097176
  44.8 0.0 copy-start.9
  44.8 0.6 copy-done.9
  45.5 0.0 copy-done.3
  45.5 0.0 copy-done.4
  45.5 60.3 %finish.1 = bf16[256,2048]{1,0:T(8,128)(2,1)} custom-call(bf16[16,32,128]{2,1,0:T(8,128)(2,1)} %bitcast.20, bf16[256,4096]{1,0:T(8,128)(2,1)} %copy-done.5, f32[256,4096]{1,0:T(8,128)} %copy-done.2, f32[32,16,128]{2,1,0:T(8,128)} %copy-done.3, f32[32,16,128]{2,1,0:T(8,128)} %copy-done.4, f32[16,32,128]{2,1,0:T(8,128)} %bitcast.22, bf16[4096,4096]{1,0:T(8,128)(2,1)} %w_out.1), custom_call_target="tpu_custom_call" | custom-call | tf_op jit(solution)/shard_map/finish/pallas_call | solution.py:272
  105.8 2.3 %copy.18 = bf16[256,2048]{1,0:T(8,128)(2,1)} copy(bf16[256,2048]{1,0:T(8,128)(2,1)} %finish.1) | data formatting | bytes 2097152
Async XLA Ops:
  0.0 3.4 %copy-start = (f32[4096,16]{0,1:T(8,128)S(1)}, f32[4096,16]{0,1:T(8,128)}, u32[]{:S(2)}) copy-start(f32[4096,16]{0,1:T(8,128)} %param.11) | copy-start | bytes 786436
  1.0 4.1 %collective-permute-start = (bf16[3,2,4096]{2,1,0:T(2,128)(2,1)S(1)}, bf16[3,2,4096]{2,1,0:T(2,128)(2,1)S(1)}, u32[]{:S(2)}, u32[]{:S(2)}) collective-permute-start(bf16[3,2,4096]{2,1,0:T(2,128)(2,1)S(1)} %slice.3), channel_id=1, source_target_pairs={{0,2},{2,4},{4,6},{6,8},{8,10},{10,12},{12,14},{14,16},{16,18},{18... | collective-permute-start | bytes 147464 | tf_op jit(solution)/shard_map/ppermute | solution.py:236
  5.1 40.4 %copy-start.3 = (f32[32,16,128]{2,1,0:T(8,128)}, f32[32,16,128]{2,1,0:T(8,128)S(1)}, u32[]{:S(2)}) copy-start(f32[32,16,128]{2,1,0:T(8,128)S(1)} %get-tuple-element.12.rate) | copy-start | bytes 786436
  5.1 40.4 %copy-start.4 = (f32[32,16,128]{2,1,0:T(8,128)}, f32[32,16,128]{2,1,0:T(8,128)S(1)}, u32[]{:S(2)}) copy-start(f32[32,16,128]{2,1,0:T(8,128)S(1)} %get-tuple-element.13.residue) | copy-start | bytes 786436
  5.1 3.0 %copy-start.1 = (bf16[3,256,4096]{2,1,0:T(8,128)(2,1)S(1)}, bf16[3,256,4096]{2,1,0:T(8,128)(2,1)}, u32[]{:S(2)}) copy-start(bf16[3,256,4096]{2,1,0:T(8,128)(2,1)} %proj.1) | copy-start | bytes 18874372
  8.1 0.9 copy-start.6
  9.1 0.9 copy-start.7
  10.0 0.9 copy-start.8
  10.9 0.7 copy-start.10
  41.5 1.9 %copy-start.2 = (f32[256,4096]{1,0:T(8,128)}, f32[256,4096]{1,0:T(8,128)S(1)}, u32[]{:S(2)}) copy-start(f32[256,4096]{1,0:T(8,128)S(1)} %get-tuple-element.10.base) | copy-start | bytes 12582916
  43.5 1.3 %copy-start.5 = (bf16[256,4096]{1,0:T(8,128)(2,1)}, bf16[256,4096]{1,0:T(8,128)(2,1)S(1)}, u32[]{:S(2)}) copy-start(bf16[256,4096]{1,0:T(8,128)(2,1)S(1)} %get-tuple-element.9.query) | copy-start | bytes 6291460
  44.8 0.7 copy-start.9

commit v3 on v2

v3 whole, which is shorter than its diff:
```python
import math

import jax
import jax.numpy as jnp
import numpy as np
from jax import lax
from jax.experimental import pallas as pl
from jax.experimental.pallas import tpu as pltpu
from jax.sharding import PartitionSpec as P

LANES = 128
SUB = 8
SPAN = 4
HALVES = 2
MESH = pl.DeviceIdType.MESH


def half_tables(block):
    k = np.arange(block)[:, None]
    t = np.arange(block)[None, :]
    angle = np.pi / (2 * block) * ((2 * k + 1) * t % (4 * block))
    fwd = np.concatenate([np.cos(angle), np.sin(angle)], axis=0)
    return jnp.asarray(fwd, jnp.bfloat16), jnp.asarray(fwd.T, jnp.bfloat16)


def spread(rows):
    return jnp.stack(
        [jnp.broadcast_to(rows[m : m + 1], (SUB, LANES)) for m in range(rows.shape[0])]
    )


def mode_weight(rates, residues, modes):
    return residues * jnp.sqrt(2.0 * rates / modes)


def fold(power):
    while power.shape[0] > 1 and power.shape[0] % 2 == 0:
        half = power.shape[0] // 2
        power = power[:half] + power[half:]
    return jnp.sum(power, axis=0)


def layer_kernel(
    proj, halo, short, rate, residue, skip, decay_rate, fwd, inv, w_out, out,
    w_buf, line, taps, prod, query, base, state, got, enter_out, enter, send, recv, own,
    w_sem, s1, r1, s2, r2, s3, r3,
):
    _, tokens, channels = proj.shape
    modes = rate.shape[1]
    count, share = got.shape[0], got.shape[1]
    parts, rank = lax.axis_size("tp"), lax.axis_index("ctx")
    me = lax.axis_index("tp")
    tiles, _, tile = w_buf.shape
    per = tiles // parts
    away = tiles - per
    width = taps.shape[1]
    group = SPAN * SUB
    row = lax.broadcasted_iota(jnp.int32, (1, SUB, LANES), 1).astype(jnp.float32)

    def load(i):
        peer = lax.rem(me + 1 + i // per, parts)
        col = pl.multiple_of((peer * per + i % per) * tile, tile)
        return pltpu.make_async_copy(w_out.at[:, pl.ds(col, tile)], w_buf.at[i], w_sem.at[i])

    @pl.loop(0, tiles)
    def _(i):
        load(i).start()

    barrier = pltpu.get_barrier_semaphore()

    @pl.loop(1, count)
    def _(o):
        pl.semaphore_signal(
            barrier, inc=1, device_id=(lax.rem(rank + o, count), me), device_id_type=MESH
        )

    @pl.loop(1, parts)
    def _(o):
        pl.semaphore_signal(
            barrier, inc=1, device_id=(rank, lax.rem(me + o, parts)), device_id_type=MESH
        )

    @pl.loop(0, channels // LANES)
    def _(j):
        lanes = pl.ds(pl.multiple_of(j * LANES, LANES), LANES)
        feats = []
        for s in range(3):
            now = proj[s, :, lanes].astype(jnp.float32)
            line[s, SUB - 2 : SUB, :] = halo[s, :, lanes].astype(jnp.float32)
            line[s, SUB : SUB + tokens, :] = now
            mixed = (
                short[s, 0:1, lanes] * now
                + short[s, 1:2, lanes] * line[s, SUB - 1 : SUB - 1 + tokens, :]
                + short[s, 2:3, lanes] * line[s, SUB - 2 : SUB - 2 + tokens, :]
            )
            feats.append(mixed.astype(jnp.bfloat16))
        query[:, lanes] = feats[0]
        product = (feats[1].astype(jnp.float32) * feats[2].astype(jnp.float32)).astype(jnp.bfloat16)
        prod[:, lanes] = product
        line[0, SUB : SUB + tokens, :] = product.astype(jnp.float32)
        rates = spread(rate[j])
        step = jnp.exp(-SUB * rates)

        def advance(i, held):
            for k in range(SPAN):
                start = pl.multiple_of(SUB + i * group + k * SUB, SUB)
                held = held * step + line[0, pl.ds(start, SUB), :][None]
            return held

        held = lax.fori_loop(0, tokens // group, advance, jnp.zeros((modes, SUB, LANES), jnp.float32))
        held = jnp.sum(held * jnp.exp(-rates * (SUB - 1 - row)), axis=1).astype(state.dtype)
        if share >= modes:
            times = share // modes
            at = pl.multiple_of((j % times) * modes, modes)
            state[j // times, pl.ds(at, modes), :] = held
        else:
            times = modes // share
            for i in range(times):
                state[j * times + i] = held[i * share : (i + 1) * share]

    pl.semaphore_wait(barrier, count + parts - 2)

    def inside(start, stop):
        @pl.loop(start, stop)
        def _(b):
            cols = pl.ds(pl.multiple_of(b * width, width), width)
            for n in range(width // LANES):
                j = b * (width // LANES) + n
                rates = spread(rate[j])
                weight = mode_weight(rates, spread(residue[j]), modes)
                step = jnp.exp(-SUB * rates)

                def advance(i, power):
                    rows = []
                    for _ in range(SPAN):
                        rows.append(fold(power))
                        power = power * step
                    at = pl.ds(pl.multiple_of(i * group, group), group)
                    taps[at, n * LANES : (n + 1) * LANES] = jnp.concatenate(rows, axis=0).astype(
                        jnp.bfloat16
                    )
                    return power

                lax.fori_loop(0, tokens // group, advance, weight * jnp.exp(-rates * row))
            here = prod[:, cols]
            sig = jnp.dot(fwd[...], here, preferred_element_type=jnp.float32)
            fil = jnp.dot(fwd[...], taps[...], preferred_element_type=jnp.float32)
            cs, ss, cf, sf = sig[:tokens], sig[tokens:], fil[:tokens], fil[tokens:]
            both = jnp.concatenate(
                [
                    (cs * cf - ss * sf).astype(jnp.bfloat16),
                    (cs * sf + ss * cf).astype(jnp.bfloat16),
                ],
                axis=0,
            )
            conv = jnp.dot(inv[...], both, preferred_element_type=jnp.float32) * (1.0 / tokens)
            base[:, cols] = conv + skip[:, cols] * here.astype(jnp.float32)

    pieces = channels // width
    def hop(src, dst, peer, slot, sent, landed):
        return pltpu.make_async_remote_copy(
            src_ref=src.at[peer], dst_ref=dst.at[slot], send_sem=sent.at[peer],
            recv_sem=landed.at[slot], device_id=(peer, me), device_id_type=MESH,
        )

    @pl.loop(1, count)
    def _(o):
        hop(state, got, lax.rem(rank + o, count), rank, s1, r1).start()

    got[rank] = state[rank]
    inside(0, pieces // 2)

    @pl.loop(1, count)
    def _(o):
        peer = lax.rem(rank + o, count)
        hop(state, got, peer, peer, s1, r1).wait()

    decay = jnp.exp(-float(tokens) * decay_rate[rank])

    def prefix(i, held):
        enter_out[i] = held.astype(enter_out.dtype)
        return held * decay + got[i].astype(jnp.float32)

    lax.fori_loop(0, count, prefix, jnp.zeros((share, LANES), jnp.float32))

    @pl.loop(1, count)
    def _(o):
        hop(enter_out, enter, lax.rem(rank + o, count), rank, s2, r2).start()

    enter[rank] = enter_out[rank]
    inside(pieces // 2, pieces)

    @pl.loop(1, count)
    def _(o):
        peer = lax.rem(rank + o, count)
        hop(enter_out, enter, peer, peer, s2, r2).wait()

    def entering(j):
        if share >= modes:
            times = share // modes
            at = pl.multiple_of((j % times) * modes, modes)
            return spread(enter[j // times, pl.ds(at, modes), :].astype(jnp.float32))
        times = modes // share
        return jnp.concatenate(
            [spread(enter[j * times + i].astype(jnp.float32)) for i in range(times)], axis=0
        )

    part = tokens // HALVES

    def gate(begin):
        @pl.loop(0, channels // LANES)
        def _(j):
            lanes = pl.ds(pl.multiple_of(j * LANES, LANES), LANES)
            rates = spread(rate[j])
            weight = mode_weight(rates, spread(residue[j]), modes)
            step = jnp.exp(-SUB * rates)

            def advance(i, power):
                rows = []
                for _ in range(SPAN):
                    rows.append(fold(power))
                    power = power * step
                at = pl.ds(pl.multiple_of(begin + i * group, group), group)
                total = jnp.concatenate(rows, axis=0) + base[at, lanes]
                query[at, lanes] = (query[at, lanes].astype(jnp.float32) * total).astype(
                    jnp.bfloat16
                )
                return power

            lax.fori_loop(
                0, part // group, advance,
                weight * jnp.exp(-rates * (row + (begin + 1.0))) * entering(j),
            )

    def give(i):
        peer = lax.rem(me + 1 + (i % away) // per, parts)
        return pltpu.make_async_remote_copy(
            src_ref=send.at[i], dst_ref=recv.at[i], send_sem=s3.at[i], recv_sem=r3.at[i],
            device_id=(rank, peer), device_id_type=MESH,
        )

    for h in range(HALVES):
        gate(h * part)

        @pl.loop(0, away)
        def _(i):
            if h == 0:
                load(i).wait()
            send[h * away + i] = jnp.dot(
                query[h * part : (h + 1) * part, :], w_buf[i], preferred_element_type=jnp.float32
            ).astype(jnp.bfloat16)
            give(h * away + i).start()

    @pl.loop(0, per)
    def _(t):
        load(away + t).wait()
        own[t] = jnp.dot(query[...], w_buf[away + t], preferred_element_type=jnp.float32)

    for h in range(HALVES):
        for t in range(per):
            total = own[t, h * part : (h + 1) * part, :]
            for o in range(parts - 1):
                give(h * away + o * per + t).wait()
                total = total + recv[h * away + o * per + t].astype(jnp.float32)
            out[h * part : (h + 1) * part, t * tile : (t + 1) * tile] = total.astype(out.dtype)


def on_device(projected, short_weight, rate, residue, skip, w_out):
    count = lax.axis_size("ctx")
    parts = lax.axis_size("tp")
    _, tokens, channels = projected.shape
    modes = rate.shape[1]
    outputs = w_out.shape[1]
    blocks = channels // LANES
    rate_b = rate.reshape(blocks, LANES, modes).transpose(0, 2, 1)
    residue_b = residue.reshape(blocks, LANES, modes).transpose(0, 2, 1)
    halo = lax.ppermute(
        projected[:, -2:, :], "ctx", [(i, i + 1) for i in range(count - 1)]
    )
    fwd, inv = half_tables(tokens)
    width = min(512, channels)
    share = blocks * modes // count
    each = outputs // parts
    tile = min(512, each)
    tiles = outputs // tile
    away = tiles - each // tile
    vmem = pl.BlockSpec(memory_space=pltpu.VMEM)
    return pl.pallas_call(
        layer_kernel,
        in_specs=[vmem] * 9 + [pl.BlockSpec(memory_space=pl.ANY)],
        out_specs=vmem,
        out_shape=jax.ShapeDtypeStruct((tokens, each), jnp.bfloat16),
        scratch_shapes=[
            pltpu.VMEM((tiles, channels, tile), jnp.bfloat16),
            pltpu.VMEM((3, tokens + SUB, LANES), jnp.float32),
            pltpu.VMEM((tokens, width), jnp.bfloat16),
            pltpu.VMEM((tokens, channels), jnp.bfloat16),
            pltpu.VMEM((tokens, channels), jnp.bfloat16),
            pltpu.VMEM((tokens, channels), jnp.float32),
            pltpu.VMEM((count, share, LANES), jnp.bfloat16),
            pltpu.VMEM((count, share, LANES), jnp.bfloat16),
            pltpu.VMEM((count, share, LANES), jnp.bfloat16),
            pltpu.VMEM((count, share, LANES), jnp.bfloat16),
            pltpu.VMEM((HALVES * away, tokens // HALVES, tile), jnp.bfloat16),
            pltpu.VMEM((HALVES * away, tokens // HALVES, tile), jnp.bfloat16),
            pltpu.VMEM((each // tile, tokens, tile), jnp.float32),
            pltpu.SemaphoreType.DMA((tiles,)),
        ]
        + [pltpu.SemaphoreType.DMA((count,))] * 4
        + [pltpu.SemaphoreType.DMA((HALVES * away,))] * 2,
        compiler_params=pltpu.CompilerParams(
            vmem_limit_bytes=61 * 2**20, collective_id=0, has_side_effects=True
        ),
        name="layer",
    )(
        projected, halo, short_weight, rate_b, residue_b, skip[None],
        rate_b.reshape(count, share, LANES), fwd, inv, w_out,
    )


def solution(mesh):
    return jax.shard_map(
        on_device,
        mesh=mesh,
        in_specs=(
            P(None, "ctx", "tp"),
            P(None, None, "tp"),
            P("tp", None),
            P("tp", None),
            P("tp"),
            P("tp", None),
        ),
        out_specs=P("ctx", "tp"),
        check_vma=False,
    )
```

time: 108 us -> 72.5 us (0.67)
  Pallas kernels: 90.1 us -> 64.1 us
  local copies, waits for them, and re-layouts: 15.5 us -> 5.84 us
    pallas_call x2 -> x1, Pallas kernels: 90.1 us -> 64.1 us  [on_device(): pl.pallas_call(layer_kernel, in_specs=[vmem] * 9 + [pl.BlockSpec(memory_s...]
    unnamed x23 -> x5, local copies, waits for them, and re-layouts: 12.7 us -> 2.93 us
  transfers between devices with their start and end apart: 1 -> 1, of which waited for: 0 -> 0; matrix products, arithmetic and copies ran while one was open for 2% -> 3% of each run, Pallas kernels for 0% -> 0%
where the time goes in v3:
time: 72.5 us; the launch traced here: 72.3 us
  Pallas kernels  64.1 us (88%)
  local copies, waits for them, and re-layouts  5.84 us (8%)
  starting transfers between devices  2.36 us (3%)
    pallas_call x1, Pallas kernels, on_device(): pl.pallas_call(layer_kernel, in_specs=[vmem] * 9 + [pl.BlockSpec(memory_s...  64.1 us
    unnamed x5, local copies, waits for them, and re-layouts  2.93 us
    ppermute x1, starting transfers between devices, on_device(): lax.ppermute(projected[:, -2:, :], 'ctx', [(i, i + 1) for i in range(coun...  2.36 us
    reshape x1, local copies, waits for them, and re-layouts, on_device(): rate_b = rate.reshape(blocks, LANES, modes).transpose(0, 2, 1)  1.89 us
  transfers between devices with their start and end apart: 1, of which 0 were waited for; matrix products, arithmetic and copies ran while one was open for 3% of the time, Pallas kernels for 0%

profile of v3, /device:TPU:0, one launch (start us, length us, event | category | flops | bytes accessed | tf_op | source)
XLA Modules:
  0.0 72.3 jit_solution(7218245145246738833)
XLA Ops:
  0.0 0.0 copy-start
  0.0 1.0 %slice.3 = bf16[3,2,4096]{2,1,0:T(2,128)(2,1)S(1)} slice(bf16[3,256,4096]{2,1,0:T(8,128)(2,1)} %proj.1), slice={[0:3], [254:256], [0:4096]} | slice | bytes 98304 | tf_op jit(solution)/shard_map/slice | solution.py:278
  1.0 2.4 %collective-permute-start = (bf16[3,2,4096]{2,1,0:T(2,128)(2,1)S(1)}, bf16[3,2,4096]{2,1,0:T(2,128)(2,1)S(1)}, u32[]{:S(2)}, u32[]{:S(2)}) collective-permute-start(bf16[3,2,4096]{2,1,0:T(2,128)(2,1)S(1)} %slice.3), channel_id=1, source_target_pairs={{0,2},{2,4},{4,6},{6,8},{8,10},{10,12},{12,14},{14,16},{16,18},{18... | collective-permute-start | bytes 147464 | tf_op jit(solution)/shard_map/ppermute | solution.py:277
  3.4 0.0 copy-done
  3.4 1.9 %copy_bitcast_fusion = (f32[32,128,16]{1,2,0:T(8,128)}, f32[32,16,128]{2,1,0:T(8,128)}, f32[32,16,128]{2,1,0:T(8,128)}) fusion(f32[4096,16]{0,1:T(8,128)S(1)} %copy-done, f32[4096,16]{0,1:T(8,128)} %param.10), kind=kLoop, calls=%fused_computation.1 | loop fusion | bytes 1310720 | tf_op jit(solution)/shard_map/reshape | solution.py:275
  5.3 0.0 collective-permute-done.halo
  5.3 0.0 copy-start.1
  5.3 0.6 copy-done.1
  5.9 64.1 %layer.1 = bf16[256,2048]{1,0:T(8,128)(2,1)} custom-call(bf16[3,256,4096]{2,1,0:T(8,128)(2,1)} %proj.1, bf16[3,2,4096]{2,1,0:T(2,128)(2,1)} %copy-done.1, f32[3,3,4096]{2,1,0:T(4,128)} %short.1, f32[32,16,128]{2,1,0:T(8,128)} %get-tuple-element.6.rate, f32[32,16,128]{2,1,0:T(8,128)} %get-tuple-element.7.residue, f32[1,4096]{1,0:T(1,128)} %bitcast.20, ...), custom_call_target="tpu_custom_call" | custom-call | tf_op jit(solution)/shard_map/layer/pallas_call | solution.py:288
  70.0 2.3 %copy.18 = bf16[256,2048]{1,0:T(8,128)(2,1)} copy(bf16[256,2048]{1,0:T(8,128)(2,1)} %layer.1) | data formatting | bytes 2097152
Async XLA Ops:
  0.0 3.4 %copy-start = (f32[4096,16]{0,1:T(8,128)S(1)}, f32[4096,16]{0,1:T(8,128)}, u32[]{:S(2)}) copy-start(f32[4096,16]{0,1:T(8,128)} %param.11) | copy-start | bytes 786436
  1.0 4.3 %collective-permute-start = (bf16[3,2,4096]{2,1,0:T(2,128)(2,1)S(1)}, bf16[3,2,4096]{2,1,0:T(2,128)(2,1)S(1)}, u32[]{:S(2)}, u32[]{:S(2)}) collective-permute-start(bf16[3,2,4096]{2,1,0:T(2,128)(2,1)S(1)} %slice.3), channel_id=1, source_target_pairs={{0,2},{2,4},{4,6},{6,8},{8,10},{10,12},{12,14},{14,16},{16,18},{18... | collective-permute-start | bytes 147464 | tf_op jit(solution)/shard_map/ppermute | solution.py:277
  5.3 0.6 copy-start.1

commit v4 on v3

--- a/solution.py
+++ b/solution.py
@@ -41,12 +41,12 @@
 
 
 def layer_kernel(
-    proj, halo, short, rate, residue, skip, decay_rate, fwd, inv, w_out, out,
-    w_buf, line, taps, prod, query, base, state, got, enter_out, enter, send, recv, own,
-    w_sem, s1, r1, s2, r2, s3, r3,
+    halo, short, rate, residue, skip, fwd, inv, proj_hbm, w_out, out,
+    proj, w_buf, line, taps, prod, query, base, state, got, enter_out, enter, send, recv, own,
+    p_sem, w_sem, s1, r1, s2, r2, s3, r3,
 ):
     _, tokens, channels = proj.shape
-    modes = rate.shape[1]
+    modes = rate.shape[0]
     count, share = got.shape[0], got.shape[1]
     parts, rank = lax.axis_size("tp"), lax.axis_index("ctx")
     me = lax.axis_index("tp")
@@ -62,6 +62,16 @@
         col = pl.multiple_of((peer * per + i % per) * tile, tile)
         return pltpu.make_async_copy(w_out.at[:, pl.ds(col, tile)], w_buf.at[i], w_sem.at[i])
 
+    chunks = p_sem.shape[0]
+    chunk = channels // chunks
+
+    def fetch(c):
+        cols = pl.ds(c * chunk, chunk)
+        return pltpu.make_async_copy(proj_hbm.at[:, :, cols], proj.at[:, :, cols], p_sem.at[c])
+
+    for c in range(chunks):
+        fetch(c).start()
+
     @pl.loop(0, tiles)
     def _(i):
         load(i).start()
@@ -80,8 +90,7 @@
             barrier, inc=1, device_id=(rank, lax.rem(me + o, parts)), device_id_type=MESH
         )
 
-    @pl.loop(0, channels // LANES)
-    def _(j):
+    def features(j):
         lanes = pl.ds(pl.multiple_of(j * LANES, LANES), LANES)
         feats = []
         for s in range(3):
@@ -98,7 +107,7 @@
         product = (feats[1].astype(jnp.float32) * feats[2].astype(jnp.float32)).astype(jnp.bfloat16)
         prod[:, lanes] = product
         line[0, SUB : SUB + tokens, :] = product.astype(jnp.float32)
-        rates = spread(rate[j])
+        rates = spread(rate[:, lanes])
         step = jnp.exp(-SUB * rates)
 
         def advance(i, held):
@@ -118,6 +127,10 @@
             for i in range(times):
                 state[j * times + i] = held[i * share : (i + 1) * share]
 
+    for c in range(chunks):
+        fetch(c).wait()
+        pl.loop(c * (chunk // LANES), (c + 1) * (chunk // LANES))(features)
+
     pl.semaphore_wait(barrier, count + parts - 2)
 
     def inside(start, stop):
@@ -126,8 +139,9 @@
             cols = pl.ds(pl.multiple_of(b * width, width), width)
             for n in range(width // LANES):
                 j = b * (width // LANES) + n
-                rates = spread(rate[j])
-                weight = mode_weight(rates, spread(residue[j]), modes)
+                lanes = pl.ds(pl.multiple_of(j * LANES, LANES), LANES)
+                rates = spread(rate[:, lanes])
+                weight = mode_weight(rates, spread(residue[:, lanes]), modes)
                 step = jnp.exp(-SUB * rates)
 
                 def advance(i, power):
@@ -175,7 +189,24 @@
         peer = lax.rem(rank + o, count)
         hop(state, got, peer, peer, s1, r1).wait()
 
-    decay = jnp.exp(-float(tokens) * decay_rate[rank])
+    if share >= modes:
+        own_rate = jnp.concatenate(
+            [
+                rate[:, pl.ds(pl.multiple_of((rank * (share // modes) + i) * LANES, LANES), LANES)]
+                for i in range(share // modes)
+            ],
+            axis=0,
+        )
+    else:
+        times = modes // share
+        at = pl.multiple_of((rank // times) * LANES, LANES)
+        column = rate[:, pl.ds(at, LANES)]
+        own_rate = column[:share]
+        for i in range(1, times):
+            own_rate = jnp.where(
+                rank % times == i, column[i * share : (i + 1) * share], own_rate
+            )
+    decay = jnp.exp(-float(tokens) * own_rate)
 
     def prefix(i, held):
         enter_out[i] = held.astype(enter_out.dtype)
@@ -211,8 +242,8 @@
         @pl.loop(0, channels // LANES)
         def _(j):
             lanes = pl.ds(pl.multiple_of(j * LANES, LANES), LANES)
-            rates = spread(rate[j])
-            weight = mode_weight(rates, spread(residue[j]), modes)
+            rates = spread(rate[:, lanes])
+            weight = mode_weight(rates, spread(residue[:, lanes]), modes)
             step = jnp.exp(-SUB * rates)
 
             def advance(i, power):
@@ -272,8 +303,6 @@
     modes = rate.shape[1]
     outputs = w_out.shape[1]
     blocks = channels // LANES
-    rate_b = rate.reshape(blocks, LANES, modes).transpose(0, 2, 1)
-    residue_b = residue.reshape(blocks, LANES, modes).transpose(0, 2, 1)
     halo = lax.ppermute(
         projected[:, -2:, :], "ctx", [(i, i + 1) for i in range(count - 1)]
     )
@@ -287,10 +316,11 @@
     vmem = pl.BlockSpec(memory_space=pltpu.VMEM)
     return pl.pallas_call(
         layer_kernel,
-        in_specs=[vmem] * 9 + [pl.BlockSpec(memory_space=pl.ANY)],
+        in_specs=[vmem] * 7 + [pl.BlockSpec(memory_space=pl.ANY)] * 2,
         out_specs=vmem,
         out_shape=jax.ShapeDtypeStruct((tokens, each), jnp.bfloat16),
         scratch_shapes=[
+            pltpu.VMEM(projected.shape, jnp.bfloat16),
             pltpu.VMEM((tiles, channels, tile), jnp.bfloat16),
             pltpu.VMEM((3, tokens + SUB, LANES), jnp.float32),
             pltpu.VMEM((tokens, width), jnp.bfloat16),
@@ -304,6 +334,7 @@
             pltpu.VMEM((HALVES * away, tokens // HALVES, tile), jnp.bfloat16),
             pltpu.VMEM((HALVES * away, tokens // HALVES, tile), jnp.bfloat16),
             pltpu.VMEM((each // tile, tokens, tile), jnp.float32),
+            pltpu.SemaphoreType.DMA((channels // width,)),
             pltpu.SemaphoreType.DMA((tiles,)),
         ]
         + [pltpu.SemaphoreType.DMA((count,))] * 4
@@ -313,8 +344,7 @@
         ),
         name="layer",
     )(
-        projected, halo, short_weight, rate_b, residue_b, skip[None],
-        rate_b.reshape(count, share, LANES), fwd, inv, w_out,
+        halo, short_weight, rate.T, residue.T, skip[None], fwd, inv, projected, w_out,
     )
 
 

time: 72.5 us -> 71.6 us (0.988)
  local copies, waits for them, and re-layouts: 5.84 us -> 3.9 us
  waiting for transfers between devices: 0.01 us -> 0.86 us
    reshape x1 -> x0, local copies, waits for them, and re-layouts: 1.89 us -> none  [on_device(): rate_b = rate.reshape(blocks, LANES, modes).transpose(0, 2, 1)]
    ppermute x1, waiting for transfers between devices: 0.01 us -> 0.86 us  [on_device(): lax.ppermute(projected[:, -2:, :], 'ctx', [(i, i + 1) for i in range(coun...]
    unnamed x5 -> x3, local copies, waits for them, and re-layouts: 2.93 us -> 2.92 us
  transfers between devices with their start and end apart: 1 -> 1, of which waited for: 0 -> 1; matrix products, arithmetic and copies ran while one was open for 3% -> 0% of each run, Pallas kernels for 0% -> 0%
where the time goes in v4:
time: 71.6 us; the launch traced here: 71.4 us
  Pallas kernels  64.2 us (90%)
  local copies, waits for them, and re-layouts  3.9 us (5%)
  starting transfers between devices  2.36 us (3%)
  waiting for transfers between devices  0.86 us (1%)
    pallas_call x1, Pallas kernels, on_device(): pl.pallas_call(layer_kernel, in_specs=[vmem] * 7 + [pl.BlockSpec(memory_s...  64.2 us
    unnamed x3, local copies, waits for them, and re-layouts  2.92 us
    ppermute x1, starting transfers between devices, on_device(): lax.ppermute(projected[:, -2:, :], 'ctx', [(i, i + 1) for i in range(coun...  2.36 us
  transfers between devices with their start and end apart: 1, of which 1 were waited for; matrix products, arithmetic and copies ran while one was open for 0% of the time, Pallas kernels for 0%

profile of v4, /device:TPU:0, one launch (start us, length us, event | category | flops | bytes accessed | tf_op | source)
XLA Modules:
  0.0 71.4 jit_solution(3396755008870460717)
XLA Ops:
  0.0 1.0 %slice.3 = bf16[3,2,4096]{2,1,0:T(2,128)(2,1)S(1)} slice(bf16[3,256,4096]{2,1,0:T(8,128)(2,1)} %proj_hbm.1), slice={[0:3], [254:256], [0:4096]} | slice | bytes 98304 | tf_op jit(solution)/shard_map/slice | solution.py:307
  1.0 2.4 %collective-permute-start = (bf16[3,2,4096]{2,1,0:T(2,128)(2,1)S(1)}, bf16[3,2,4096]{2,1,0:T(2,128)(2,1)S(1)}, u32[]{:S(2)}, u32[]{:S(2)}) collective-permute-start(bf16[3,2,4096]{2,1,0:T(2,128)(2,1)S(1)} %slice.3), channel_id=1, source_target_pairs={{0,2},{2,4},{4,6},{6,8},{8,10},{10,12},{12,14},{14,16},{16,18},{18... | collective-permute-start | bytes 147464 | tf_op jit(solution)/shard_map/ppermute | solution.py:306
  3.4 0.9 %collective-permute-done.halo = bf16[3,2,4096]{2,1,0:T(2,128)(2,1)S(1)} collective-permute-done((bf16[3,2,4096]{2,1,0:T(2,128)(2,1)S(1)}, bf16[3,2,4096]{2,1,0:T(2,128)(2,1)S(1)}, u32[]{:S(2)}, u32[]{:S(2)}) %collective-permute-start) | collective-permute-done | bytes 49184 | tf_op jit(solution)/shard_map/ppermute | solution.py:306
  4.2 0.0 copy-start
  4.2 0.6 copy-done
  4.8 64.2 %layer.1 = bf16[256,2048]{1,0:T(8,128)(2,1)} custom-call(bf16[3,2,4096]{2,1,0:T(2,128)(2,1)} %copy-done, f32[3,3,4096]{2,1,0:T(4,128)} %short.1, f32[16,4096]{1,0:T(8,128)} %bitcast.3, f32[16,4096]{1,0:T(8,128)} %bitcast.4, f32[1,4096]{1,0:T(1,128)} %bitcast.5, bf16[512,256]{1,0:T(8,128)(2,1)} %constant.4.clone.fwd, bf16[256,512]{1,0:T(8,128)(2,1)} %constant.5.clone.inv, ...), custom_call_target="tpu_custom_call" | custom-call | tf_op jit(solution)/shard_map/layer/pallas_call | solution.py:317
  69.1 2.3 %copy.10 = bf16[256,2048]{1,0:T(8,128)(2,1)} copy(bf16[256,2048]{1,0:T(8,128)(2,1)} %layer.1) | data formatting | bytes 2097152
Async XLA Ops:
  1.0 3.2 %collective-permute-start = (bf16[3,2,4096]{2,1,0:T(2,128)(2,1)S(1)}, bf16[3,2,4096]{2,1,0:T(2,128)(2,1)S(1)}, u32[]{:S(2)}, u32[]{:S(2)}) collective-permute-start(bf16[3,2,4096]{2,1,0:T(2,128)(2,1)S(1)} %slice.3), channel_id=1, source_target_pairs={{0,2},{2,4},{4,6},{6,8},{8,10},{10,12},{12,14},{14,16},{16,18},{18... | collective-permute-start | bytes 147464 | tf_op jit(solution)/shard_map/ppermute | solution.py:306
  4.2 0.6 copy-start
